TPU v7x, 512 devices: a whole 4x4x16 slice. The times are simulated.
512 devices in a mesh: tok: 16 (over y, x), own: 32 (over z, core).
Axes of the slice: x: 4, y: 4, z: 16, core: 2. Of those that a mesh axis runs over, the one named last changes fastest.
Arguments:
- hidden: bfloat16 [2048, 24576], P('tok', 'own'), may hold values from -6 to 6
- grad_out: bfloat16 [2048, 6144], P('tok', 'own'), may hold values from -6 to 6
- old_weight: bfloat16 [768, 128, 128], P('own'), may hold values from -6 to 6
- old_first: bfloat16 [768, 128, 128], P('own'), may hold values from -1.5 to 1.5
- old_second: bfloat16 [768, 128, 128], P('own'), may hold values from 0.0049743652 to 0.19921875
- old_blocks: int32 [768, 2], replicated, may hold values from 0 to 191, as said below
- new_blocks: int32 [768, 2], replicated, may hold values from 0 to 191, as said below
- new_owner: int32 [768], replicated, may hold values from 0 to 31, as said below
Outputs:
- output: bfloat16 [2048, 6144], P('tok', 'own')
- new_weight: bfloat16 [768, 128, 128], P('own')
- new_first: bfloat16 [768, 128, 128], P('own')
- new_second: bfloat16 [768, 128, 128], P('own')
Inputs may be any that keep to these rules, and one draw needn't show every extreme that they name: `old_blocks`: rows are (row block of the 24576 inputs, column block of the 6144 outputs); the old blocks are distinct, and each new entry is either the old block of that slot or a block found in neither list elsewhere. `new_blocks`: same form as old_blocks; the new blocks are distinct. Of the 24 blocks that one new owner receives, at most 1 has its row block among the 24576 / 32 input features held by any one device along own, and this bound of 1 is reached in every draw. `new_owner`: every owner receives exactly 24 blocks; the slots of one old owner send at most 1 block to one new owner, and 1 is reached in every draw.
All inputs are finite; a program needn't handle non-finite values.
Results may differ from a plain program's by a relative error of at most 0.022.
Values may be sent and summed in bfloat16 or wider, within the bound.
A program may use at most 64 MiB of HBM per device.

v0:
```python
import jax
import jax.numpy as jnp
from jax import lax
from jax.sharding import PartitionSpec as P

beta_one = 0.9
beta_two = 0.95
rate = 0.1
epsilon = 0.1
fix_one = 1.0 - 0.9**10
fix_two = 1.0 - 0.95**10


def adam_update(weight, first, second, grad):
    moment = beta_one * first.astype(jnp.float32) + (1.0 - beta_one) * grad
    square = beta_two * second.astype(jnp.float32) + (1.0 - beta_two) * grad * grad
    change = rate * (moment / fix_one) / (jnp.sqrt(square / fix_two) + epsilon)
    updated = weight.astype(jnp.float32) - change
    return (updated.astype(jnp.bfloat16), moment.astype(jnp.bfloat16), square.astype(jnp.bfloat16))


def local(hidden, grad_out, old_weight, old_first, old_second, old_blocks, new_blocks, new_owner):
    owners = lax.axis_size("own")
    me = lax.axis_index("own")
    per_dev = old_weight.shape[0]
    block = old_weight.shape[1]
    total = old_blocks.shape[0]
    width = grad_out.shape[1] * owners
    tokens = hidden.shape[0]
    capacity = -(-per_dev // owners)
    scale = (total * block * block / width) ** (-0.5)
    kept = ((old_blocks[:, 0] == new_blocks[:, 0]) & (old_blocks[:, 1] == new_blocks[:, 1])).astype(
        jnp.int32
    )
    onehot = (new_owner[:, None] == jnp.arange(owners, dtype=jnp.int32)[None, :]).astype(jnp.int32)
    before = jnp.cumsum(onehot, 0) - onehot
    rank = jnp.sum(before * onehot, 1)
    slot = new_owner * per_dev + rank
    dests = new_owner.reshape(owners, per_dev)
    positions = jnp.arange(per_dev, dtype=jnp.int32)
    earlier = positions[None, :] < positions[:, None]
    same = (dests[:, :, None] == dests[:, None, :]) & earlier[None, :, :]
    pair_rank = jnp.sum(same.astype(jnp.int32), 2).reshape(total)
    base = me * per_dev
    local_dest = lax.dynamic_slice_in_dim(new_owner, base, per_dev)
    local_pair = lax.dynamic_slice_in_dim(pair_rank, base, per_dev)
    local_kept = lax.dynamic_slice_in_dim(kept, base, per_dev)
    buffer_slots = jnp.arange(owners * capacity, dtype=jnp.int32)
    send_index = local_dest * capacity + local_pair
    send_pick = (
        (send_index[None, :] == buffer_slots[:, None]) & (local_kept[None, :] == 1)
    ).astype(jnp.bfloat16)
    source_index = jnp.arange(total, dtype=jnp.int32) // per_dev * capacity + pair_rank
    mine = (slot[None, :] == base + positions[:, None]).astype(jnp.int32)
    from_index = jnp.sum(mine * source_index[None, :], 1)
    take_pick = (from_index[:, None] == buffer_slots[None, :]).astype(jnp.bfloat16)
    rows_new = jnp.sum(mine * new_blocks[:, 0][None, :], 1)
    cols_new = jnp.sum(mine * new_blocks[:, 1][None, :], 1)
    stacked = jnp.stack([old_weight, old_first, old_second], 1)
    flat = stacked.reshape(per_dev, -1)
    outgoing = jnp.dot(send_pick, flat, preferred_element_type=jnp.float32).astype(jnp.bfloat16)
    arrived = lax.all_to_all(
        outgoing.reshape((owners, capacity) + stacked.shape[1:]),
        "own",
        split_axis=0,
        concat_axis=0,
        tiled=True,
    )
    flat = arrived.reshape(owners * capacity, -1)
    placed_rows = jnp.dot(take_pick, flat, preferred_element_type=jnp.float32).astype(jnp.bfloat16)
    state = placed_rows.reshape((per_dev,) + arrived.shape[2:])
    weight = state[:, 0]
    gathered = lax.all_gather(hidden, "own", axis=1, tiled=True)
    picked = jnp.take(gathered.reshape(tokens, -1, block), rows_new, axis=1)
    product = jnp.einsum("tjk,jkl->tjl", picked, weight, preferred_element_type=jnp.float32) * scale
    placed = (cols_new[:, None] == jnp.arange(width // block, dtype=jnp.int32)[None, :]).astype(
        jnp.float32
    )
    partial_value = jnp.einsum("tjl,jc->tcl", product, placed).reshape(tokens, width)
    output = lax.psum_scatter(
        partial_value.astype(jnp.bfloat16), "own", scatter_dimension=1, tiled=True
    )
    cotangent = lax.all_gather(grad_out, "own", axis=1, tiled=True)
    cot_picked = jnp.take(cotangent.reshape(tokens, -1, block), cols_new, axis=1)
    grad = (
        jnp.einsum("tjk,tjl->jkl", picked, cot_picked, preferred_element_type=jnp.float32) * scale
    )
    grad_sum = lax.psum(grad.astype(jnp.bfloat16), "tok").astype(jnp.float32)
    new_weight, new_first, new_second = adam_update(state[:, 0], state[:, 1], state[:, 2], grad_sum)
    return (output, new_weight, new_first, new_second)


def solution(mesh):
    in_specs = (
        P("tok", "own"),
        P("tok", "own"),
        P("own", None, None),
        P("own", None, None),
        P("own", None, None),
        P(),
        P(),
        P(),
    )
    out_specs = (P("tok", "own"), P("own", None, None), P("own", None, None), P("own", None, None))
    return jax.shard_map(local, mesh=mesh, in_specs=in_specs, out_specs=out_specs, check_vma=False)
```

profile of v0, /device:TPU:1, one launch (start us, length us, event | category | flops | bytes accessed | tf_op | source)
XLA Modules:
  0.0 476.2 jit_solution(8632343769588433032)
XLA Ops:
  7.2 0.0 all-gather.5.cloned.1.call-start
  7.2 0.7 all-gather.5.cloned.1.call-update
  7.9 0.0 all-gather.3.cloned.1.call-start
  7.9 1.7 copy.81
  9.7 0.0 all-gather.3.cloned.1.call-update
  9.7 0.8 slice_reduce_fusion.4
  10.5 0.8 eq.113
  11.3 0.1 copy.75
  11.4 0.2 convert_reduce_fusion
  11.5 0.1 copy.77
  11.6 0.1 reshape.135
  11.7 0.8 slice_reduce_fusion.3
  12.5 0.8 dynamic-slice_add_fusion
  13.3 1.9 pad_maximum_fusion
  15.1 0.1 dynamic-slice_compare_fusion
  15.2 0.3 copy.78
  15.5 1.8 fusion.4
  17.3 2.4 copy.103
  19.7 0.0 copy-start.3
  19.7 16.9 %all-to-all-start = ((bf16[32,1,3,128,128]{4,3,2,1,0:T(8,128)(2,1)}), bf16[32,1,3,128,128]{4,3,2,1,0:T(8,128)(2,1)S(1)}, u32[]{:S(2)}, u32[]{:S(2)}) async-start(bf16[32,1,3,128,128]{4,3,2,1,0:T(8,128)(2,1)} %bitcast.6), calls=%async_computation | async-start | bytes 6291456 | tf_op jit(solution)/shard_map/all_to_all | solution.py:62
  36.6 0.0 all-reduce.2.cloned.1.call-start
  36.7 0.0 copy-done.3
  36.7 1.8 reduce-window.6
  38.4 0.3 slice_reduce_fusion
  38.7 0.1 fusion.27
  38.9 0.2 fusion.29
  39.2 73.0 %all-gather.5.cloned.1.call-done = bf16[128,6144]{0,1:T(8,128)(2,1)} async-done(((bf16[128,192]{0,1:T(8,128)(2,1)}), bf16[128,6144]{0,1:T(8,128)(2,1)}) %all-gather.5.cloned.1.call-update) | async-done | bytes 1572880 | tf_op jit(solution)/shard_map/all_gather | solution.py:83
  112.2 2.7 copy.87
  114.8 3.0 gather_fusion.1
  117.8 114.1 %all-gather.3.cloned.1.call-done = bf16[128,24576]{0,1:T(8,128)(2,1)} async-done(((bf16[128,768]{0,1:T(8,128)(2,1)}), bf16[128,24576]{0,1:T(8,128)(2,1)}) %all-gather.3.cloned.1.call-update) | async-done | bytes 6291472 | tf_op jit(solution)/shard_map/all_gather | solution.py:73
  231.9 8.6 %copy.82 = bf16[128,192,128]{2,0,1:T(8,128)(2,1)} copy(bf16[128,192,128]{0,2,1:T(8,128)(2,1)} %bitcast.96) | data formatting | bytes 12582912 | tf_op jit(solution)/shard_map/reshape | solution.py:74
  240.5 4.3 gather_fusion
  244.9 2.8 multiply_convert_fusion
  247.7 0.0 all-reduce.2.cloned.1.call-update
  247.7 0.2 reduce-scatter.2.cloned.1.call-start
  247.9 0.0 all-to-all-done
  247.9 1.9 fusion.7
  249.9 0.0 copy-start.2
  249.9 0.5 copy.105
  250.4 0.6 copy-done.2
  251.0 0.4 multiply_bitcast_fusion
  251.4 2.0 fusion.13
  253.4 2.9 copy.97
  256.3 0.0 reduce-scatter.2.cloned.1.call-update
  256.3 1.3 fusion.49
  257.6 0.0 copy-start
  257.6 1.6 copy.100
  259.2 0.0 copy-done
  259.2 0.4 copy.99
  259.6 0.4 copy.98
  260.0 99.1 %all-reduce.2.cloned.1.call-done = bf16[24,128,128]{1,2,0:T(8,128)(2,1)} async-done(((bf16[24,128,128]{1,2,0:T(8,128)(2,1)}), bf16[24,128,128]{1,2,0:T(8,128)(2,1)}) %all-reduce.2.cloned.1.call-update) | async-done | bytes 786448 | tf_op jit(solution)/shard_map/psum | solution.py:88
  359.1 3.6 fusion.17
  362.7 0.0 copy-start.1
  362.7 2.4 copy.91
  365.1 0.0 copy-done.1
  365.1 1.2 copy.92
  366.2 1.2 copy.93
  367.4 102.2 %reduce-scatter.2.cloned.1.call-done = bf16[128,192]{0,1:T(8,128)(2,1)} async-done(((bf16[128,6144]{0,1:T(8,128)(2,1)}), bf16[128,192]{0,1:T(8,128)(2,1)}) %reduce-scatter.2.cloned.1.call-update) | async-done | bytes 49168 | tf_op jit(solution)/shard_map/reduce_scatter | solution.py:80
  (12 shorter events, 0.1 us)
Async XLA Ops:
  7.2 105.0 %all-gather.5.cloned.1.call-start = ((), (), s32[]{:S(2)}) async-start(), calls=%async_computation.4 | async-start | bytes 1622016 | tf_op jit(solution)/shard_map/all_gather | solution.py:83
  7.9 224.0 %all-gather.3.cloned.1.call-start = ((), (), s32[]{:S(2)}) async-start(), calls=%async_computation.2 | async-start | bytes 6488064 | tf_op jit(solution)/shard_map/all_gather | solution.py:73
  19.7 16.9 %copy-start.3 = (s32[768]{0:T(1024)S(1)}, s32[768]{0:T(1024)}, u32[]{:S(2)}) copy-start(s32[768]{0:T(1024)} %param.15) | copy-start | bytes 9220
  19.7 228.2 %all-to-all-start = ((bf16[32,1,3,128,128]{4,3,2,1,0:T(8,128)(2,1)}), bf16[32,1,3,128,128]{4,3,2,1,0:T(8,128)(2,1)S(1)}, u32[]{:S(2)}, u32[]{:S(2)}) async-start(bf16[32,1,3,128,128]{4,3,2,1,0:T(8,128)(2,1)} %bitcast.6), calls=%async_computation | async-start | bytes 6291456 | tf_op jit(solution)/shard_map/all_to_all | solution.py:62
  36.6 322.5 %all-reduce.2.cloned.1.call-start = ((), (), s32[]{:S(2)}) async-start(), calls=%async_computation.5 | async-start | bytes 1572864 | tf_op jit(solution)/shard_map/psum | solution.py:88
  247.7 221.9 %reduce-scatter.2.cloned.1.call-start = ((), (), s32[]{:S(2)}) async-start(), calls=%async_computation.3 | async-start | bytes 1622016 | tf_op jit(solution)/shard_map/reduce_scatter | solution.py:80
  249.9 1.1 copy-start.2
  257.6 1.6 copy-start
  362.7 2.4 copy-start.1
Sparse Core Ops, SparseCore 0:
  10.1 101.9 all-gather.4
  114.9 117.0 all-gather.2
  247.8 111.2 all-reduce.1
  362.5 107.0 reduce-scatter.1
where the time goes:
time: 479 us; the launch traced here: 476 us
  waiting for transfers between devices  389 us (81%)
  local copies, waits for them, and re-layouts  38.2 us (8%)
  starting transfers between devices  17.2 us (4%)
  between operations  14 us (3%)
  matrix products  8.96 us (2%)
  other arithmetic  8.68 us (2%)
    all_gather x1, waiting for transfers between devices, local(): gathered = lax.all_gather(hidden, 'own', axis=1, tiled=True)  114 us
    reduce_scatter x1, waiting for transfers between devices, local(): lax.psum_scatter(partial_value.astype(jnp.bfloat16), 'own', scatter_dimen...  102 us
    psum x1, waiting for transfers between devices, local(): grad_sum = lax.psum(grad.astype(jnp.bfloat16), 'tok').astype(jnp.float32)  99.1 us
    all_gather x1, waiting for transfers between devices, local(): cotangent = lax.all_gather(grad_out, 'own', axis=1, tiled=True)  73 us
    all_to_all x1, starting transfers between devices, local(): lax.all_to_all(outgoing.reshape((owners, capacity) + stacked.shape[1:]),...  16.9 us
    unnamed x17, local copies, waits for them, and re-layouts  12.3 us
  transfers between devices with their start and end apart: 5, of which 4 were waited for; matrix products, arithmetic and copies ran while one was open for 12% of the time, Pallas kernels for 0%

commit v1 on v0

v1 whole, which is shorter than its diff:
```python
import functools

import jax
import jax.numpy as jnp
from jax import lax
from jax.experimental import pallas as pl
from jax.experimental.pallas import tpu as pltpu
from jax.sharding import PartitionSpec as P

MESH = pl.DeviceIdType.MESH

beta_one = 0.9
beta_two = 0.95
rate = 0.1
epsilon = 0.1
fix_one = 1.0 - 0.9**10
fix_two = 1.0 - 0.95**10

BLOCK = 128
ROWS = 8
F32 = jnp.float32
BF16 = jnp.bfloat16


SEND_SLOT = 0
ROW_TILE, ROW_ODD, ROW_KEPT, ROW_ROW, ROW_COL = 1, 2, 3, 4, 5
NEW_TILE, NEW_ODD, NEW_OLD, NEW_ROW, NEW_KEPT = 6, 7, 8, 9, 10
CELL = 11
TABLE_ROWS = 24


def table_kernel(owners, per_dev, row_share, lists_ref, table_ref):
    me = lax.axis_index("own")
    total = lists_ref.shape[0]
    shape = (total, 128)

    def column(i):
        return jnp.broadcast_to(lists_ref[:, i : i + 1], shape)

    owner, old_row, old_col, new_row, new_col = [column(i) for i in range(5)]
    kept = ((old_row == new_row) & (old_col == new_col)).astype(jnp.int32)
    index = lax.broadcasted_iota(jnp.int32, shape, 0)
    lane = lax.broadcasted_iota(jnp.int32, shape, 1)
    row_in = new_row - me * row_share
    row_mine = (row_in >= 0) & (row_in < row_share)
    zero = jnp.zeros(shape, jnp.int32)

    def pick(where, value):
        return jnp.sum(jnp.where(where, value, zero), axis=0, keepdims=True)

    def put(row, value):
        table_ref[row : row + 1, :] = value

    table_ref[...] = jnp.zeros_like(table_ref)
    local = index - me * per_dev
    put(SEND_SLOT, pick((owner == lane) & (local >= 0) & (local < per_dev), local))

    code = ((index * 2 + kept) * 64 + new_col) * 256
    at_row = pick((owner == lane) & row_mine, code + row_in)
    put(ROW_TILE, at_row >> 16)
    put(ROW_ODD, (at_row >> 15) & 1)
    put(ROW_KEPT, (at_row >> 14) & 1)
    put(ROW_COL, (at_row >> 8) & 63)
    put(ROW_ROW, at_row & 255)

    down = lax.broadcasted_iota(jnp.int32, (total, total), 0)
    across = lax.broadcasted_iota(jnp.int32, (total, total), 1)
    earlier = jnp.where(across < down, 1.0, 0.0).astype(BF16)
    mine = owner == me
    rank = jnp.dot(earlier, jnp.where(mine, 1.0, 0.0).astype(BF16), preferred_element_type=F32)
    at_new = pick(mine & (rank.astype(jnp.int32) == lane), (index * 2 + kept) * 256 + new_row)
    new_index = at_new >> 9
    put(NEW_TILE, at_new >> 10)
    put(NEW_ODD, (at_new >> 9) & 1)
    put(NEW_KEPT, (at_new >> 8) & 1)
    old_owner = jnp.zeros_like(at_new)
    row_owner = jnp.zeros_like(at_new)
    for i in range(1, owners):
        old_owner += (new_index >= i * per_dev).astype(jnp.int32)
        row_owner += ((at_new & 255) >= i * row_share).astype(jnp.int32)
    put(NEW_OLD, old_owner)
    put(NEW_ROW, row_owner)

    for r in range(row_share):
        put(CELL + r, owners + pick((row_in == r) & (new_col == lane), owner - owners))


def adam_update(weight, first, second, grad):
    moment = beta_one * first + (1.0 - beta_one) * grad
    square = beta_two * second + (1.0 - beta_two) * grad * grad
    change = rate * (moment / fix_one) / (jnp.sqrt(square / fix_two) + epsilon)
    return weight - change, moment, square


def step_kernel(
    scale,
    table,
    cot,
    hid,
    old_w,
    old_m,
    old_v,
    out_y,
    out_w,
    out_m,
    out_v,
    loc,
    pairs,
    mv_out,
    mv_in,
    cot_all,
    w_all,
    cot_blk,
    hid_t,
    g_out,
    g_in,
    g_sum,
    g_new,
    w_xy,
    w_blk,
    part,
    part_sib,
    right_out,
    right_in,
    left_out,
    left_in,
    fin,
    state,
    loc_sem,
    ring_send,
    ring_recv,
    sib_send,
    sib_recv,
    z_send,
    z_recv,
    xy_send,
    xy_recv,
    rs_send,
    rs_recv,
    pair_send,
    pair_recv,
):
    toks, owners = lax.axis_size("tok"), lax.axis_size("own")
    chips = owners // 2
    t, o = lax.axis_index("tok"), lax.axis_index("own")
    z, core = o // 2, o % 2
    right = {"tok": t, "own": ((z + 1) % chips) * 2 + core}
    left = {"tok": t, "own": ((z + chips - 1) % chips) * 2 + core}
    sibling = {"tok": t, "own": z * 2 + 1 - core}
    per_dev = old_w.shape[0]
    half_dev = per_dev // 2
    row_share = hid_t.shape[0]
    cols = cot_blk.shape[0]
    chunk = cols // chips
    half = BLOCK // 2

    def remote(src, dst, send, recv, device):
        return pltpu.make_async_remote_copy(
            src_ref=src, dst_ref=dst, send_sem=send, recv_sem=recv, device_id=device, device_id_type=MESH
        )

    rows = pl.ds((t // 2) * 16, 16)
    local = [
        pltpu.make_async_copy(old.at[:, rows, :], loc.at[i], loc_sem.at[i])
        for i, old in enumerate((old_w, old_m, old_v))
    ]
    for copy in local:
        copy.start()
    barrier = pltpu.get_barrier_semaphore()

    def greet_z(d, carry):
        pl.semaphore_signal(barrier, inc=1, device_id={"tok": t, "own": (o + d) % owners}, device_id_type=MESH)
        return carry

    def greet_xy(d, carry):
        pl.semaphore_signal(barrier, inc=1, device_id={"tok": (t + d) % toks, "own": o}, device_id_type=MESH)
        return carry

    lax.fori_loop(1, owners, greet_z, 0)
    lax.fori_loop(1, toks, greet_xy, 0)

    cot_all[o] = cot[...]
    for copy in local:
        copy.wait()
    odd_rows = (jnp.zeros((ROWS, BLOCK), jnp.int32) + t % 2) == 1

    def own_rows(i, k):
        both = loc[i, k].astype(F32)
        return jnp.where(odd_rows, both[ROWS:], both[:ROWS])

    def pack_w(p, carry):
        w_all[o * half_dev + p] = jnp.concatenate([own_rows(0, 2 * p), own_rows(0, 2 * p + 1)], 0).astype(BF16)
        return carry

    lax.fori_loop(0, half_dev, pack_w, 0)
    pl.semaphore_wait(barrier, owners - 1 + toks - 1)

    steps = ((chips // 2, chips - 1 - chips // 2), (chips - 1 - chips // 2, chips // 2))

    def shard(b, zz, cc):
        own = (zz % chips) * 2 + cc
        return cot_all.at[own] if b == 0 else w_all.at[pl.ds(own * half_dev, half_dev)]

    def hop(b, way, k):
        zz = z + chips - k if way == 0 else z + k
        ref = shard(b, zz, core)
        return remote(
            ref, ref, ring_send.at[b, way, k], ring_recv.at[b, way, k], right if way == 0 else left
        )

    def aside(b, way, k):
        zz = z + chips - k if way == 0 else z + k
        ref = shard(b, zz, core)
        return remote(ref, ref, sib_send.at[b, way, k], sib_recv.at[b, way, k], sibling)

    for b in range(2):
        for way in range(2):
            if steps[b][way] > 0:
                hop(b, way, 0).start()
    for b in range(2):
        aside(b, 0, 0).start()

    def pack_mv(k, carry):
        pairs[k] = jnp.concatenate([own_rows(1, k), own_rows(2, k)], 0).astype(BF16)
        return carry

    lax.fori_loop(0, per_dev, pack_mv, 0)

    def pick_mv(n, carry):
        mv_out[n] = pairs[table[SEND_SLOT, n]]
        return carry

    lax.fori_loop(0, owners, pick_mv, 0)
    mv_in[o] = mv_out[o]
    for r in range(row_share):
        hid_t[r] = hid[:, r * BLOCK : (r + 1) * BLOCK].astype(F32).T.astype(BF16)
    w_blk[owners] = jnp.zeros((BLOCK, BLOCK), BF16)

    for k in range(chips // 2):
        for b in range(2):
            for way in range(2):
                if k < steps[b][way]:
                    hop(b, way, k).wait_recv()
                    if k + 1 < steps[b][way]:
                        hop(b, way, k + 1).start()
                    aside(b, way, k + 1).start()

    def mv_copy(d):
        to = (o + d) % owners
        return remote(
            mv_out.at[to], mv_in.at[o], z_send.at[0, d], z_recv.at[0, d], {"tok": t, "own": to}
        )

    def start_mv(d, carry):
        mv_copy(d).start()
        return carry

    lax.fori_loop(1, owners, start_mv, 0)

    def wait_aside(b):
        aside(b, 0, 0).wait_recv()
        for way in range(2):
            for k in range(steps[b][way]):
                aside(b, way, k + 1).wait_recv()

    wait_aside(0)
    low = lax.broadcasted_iota(jnp.int32, (half, BLOCK), 1) < half

    def lay_cot(zz, carry):
        first, last = cot_all[2 * zz], cot_all[2 * zz + 1]
        cot_blk[3 * zz] = first[:BLOCK]
        cot_blk[3 * zz + 2] = last[:BLOCK]
        a, b = first[BLOCK:].astype(F32), last[BLOCK:].astype(F32)
        top = jnp.where(low, a, pltpu.roll(b, half, 1))
        bottom = jnp.where(low, pltpu.roll(a, half, 1), b)
        cot_blk[3 * zz + 1] = jnp.concatenate([top, bottom], 0).astype(BF16)
        return carry

    lax.fori_loop(0, chips, lay_cot, 0)

    def grad_pair(k, carry):
        slices = []
        for n in (2 * k, 2 * k + 1):
            g = jnp.dot(hid_t[table[ROW_ROW, n]], cot_blk[table[ROW_COL, n]], preferred_element_type=F32)
            slices.append((g * scale).reshape(toks, ROWS, BLOCK))
        g_out[:, k] = jnp.concatenate(slices, 1).astype(BF16)
        return carry

    lax.fori_loop(0, owners // 2, grad_pair, 0)

    def g_copy(d):
        to = (t + d) % toks
        return remote(g_out.at[to], g_in.at[t], xy_send.at[0, d], xy_recv.at[0, d], {"tok": to, "own": o})

    def start_g(d, carry):
        g_copy(d).start()
        return carry

    lax.fori_loop(1, toks, start_g, 0)
    g_in[t] = g_out[t]

    wait_aside(1)

    def rows_of(tile, odd):
        both = w_all[tile].astype(F32)
        return jnp.where((jnp.zeros((ROWS, BLOCK), jnp.int32) + odd) == 1, both[ROWS:], both[:ROWS])

    def pick_w(k, carry):
        parts = []
        for n in (2 * k, 2 * k + 1):
            parts.append(rows_of(table[ROW_TILE, n], table[ROW_ODD, n]) * table[ROW_KEPT, n].astype(F32))
        w_xy[t, k] = jnp.concatenate(parts, 0).astype(BF16)
        return carry

    lax.fori_loop(0, owners // 2, pick_w, 0)

    def w_copy(d):
        to = (t + d) % toks
        return remote(w_xy.at[t], w_xy.at[t], xy_send.at[1, d], xy_recv.at[1, d], {"tok": to, "own": o})

    def start_w(d, carry):
        w_copy(d).start()
        return carry

    lax.fori_loop(1, toks, start_w, 0)

    def wait_g(d, carry):
        g_copy(d).wait_recv()
        return carry

    lax.fori_loop(1, toks, wait_g, 0)

    def sum_g(k, carry):
        total = jnp.sum(g_in[:, k].astype(F32), axis=0)
        g_sum[2 * k] = total[:ROWS]
        g_sum[2 * k + 1] = total[ROWS:]
        return carry

    lax.fori_loop(0, owners // 2, sum_g, 0)

    def gz_copy(d):
        to = (o + d) % owners
        return remote(
            g_sum.at[to], g_new.at[o], z_send.at[1, d], z_recv.at[1, d], {"tok": t, "own": to}
        )

    def start_gz(d, carry):
        gz_copy(d).start()
        return carry

    lax.fori_loop(1, owners, start_gz, 0)
    g_new[o] = g_sum[o]

    def wait_w(d, carry):
        w_copy(d).wait_recv()
        return carry

    lax.fori_loop(1, toks, wait_w, 0)

    def lay_w(k, carry):
        both = w_xy[:, k].astype(F32)
        w_blk[2 * k] = both[:, :ROWS].reshape(BLOCK, BLOCK).astype(BF16)
        w_blk[2 * k + 1] = both[:, ROWS:].reshape(BLOCK, BLOCK).astype(BF16)
        return carry

    lax.fori_loop(0, owners // 2, lay_w, 0)

    def product(q, carry):
        total = jnp.zeros((BLOCK, 2 * BLOCK), F32)
        for r in range(0, row_share, 2):
            wide = jnp.concatenate(
                [
                    jnp.concatenate([w_blk[table[CELL + r + i, 2 * q + j]] for j in range(2)], 1)
                    for i in range(2)
                ],
                0,
            )
            total += jnp.dot(hid[:, r * BLOCK : (r + 2) * BLOCK], wide, preferred_element_type=F32)
        total = (total * scale).astype(BF16)
        for i in range(2):
            for j in range(2):
                part[i, 2 * q + j] = total[i * half : (i + 1) * half, j * BLOCK : (j + 1) * BLOCK]
        return carry

    lax.fori_loop(0, cols // 2, product, 0)
    swap = remote(part.at[1 - core], part_sib, pair_send.at[0], pair_recv.at[0], sibling)
    swap.start()

    def wait_z(d, carry):
        mv_copy(d).wait_recv()
        gz_copy(d).wait_recv()
        return carry

    lax.fori_loop(1, owners, wait_z, 0)

    def adam_pair(p, carry):
        results = []
        for s in (2 * p, 2 * p + 1):
            kept = table[NEW_KEPT, s].astype(F32)
            w = rows_of(table[NEW_TILE, s], table[NEW_ODD, s]) * kept
            both = mv_in[table[NEW_OLD, s]].astype(F32) * kept
            results.append(adam_update(w, both[:ROWS], both[ROWS:], g_new[table[NEW_ROW, s]]))
        for i in range(3):
            state[t, i, p] = jnp.concatenate([r[i] for r in results], 0).astype(BF16)
        return carry

    lax.fori_loop(0, half_dev, adam_pair, 0)

    def state_copy(i, d):
        to = (t + d) % toks
        return remote(
            state.at[t, i], state.at[t, i], xy_send.at[2 + i, d], xy_recv.at[2 + i, d], {"tok": to, "own": o}
        )

    for i in range(3):

        def start_state(d, carry, i=i):
            state_copy(i, d).start()
            return carry

        lax.fori_loop(1, toks, start_state, 0)

    swap.wait_recv()

    def term(zz):
        at = pl.ds((zz % chips) * chunk, chunk)
        return part[core, at].astype(F32) + part_sib[at].astype(F32)

    to_right, to_left = steps[0]

    def rs_copy(way, k):
        if way == 0:
            return remote(right_out.at[k], right_in.at[k], rs_send.at[0, k], rs_recv.at[0, k], right)
        return remote(left_out.at[k], left_in.at[k], rs_send.at[1, k], rs_recv.at[1, k], left)

    for k in range(to_right):
        value = term(z + to_right - k)
        if k > 0:
            rs_copy(0, k - 1).wait_recv()
            value += right_in[k - 1].astype(F32)
        right_out[k] = value.astype(BF16)
        rs_copy(0, k).start()
        if k < to_left:
            value = term(z + chips - to_left + k)
            if k > 0:
                rs_copy(1, k - 1).wait_recv()
                value += left_in[k - 1].astype(F32)
            left_out[k] = value.astype(BF16)
            rs_copy(1, k).start()
    value = term(z)
    rs_copy(0, to_right - 1).wait_recv()
    value += right_in[to_right - 1].astype(F32)
    if to_left > 0:
        rs_copy(1, to_left - 1).wait_recv()
        value += left_in[to_left - 1].astype(F32)
    fin[core] = value.astype(BF16)
    finish = remote(fin.at[core], fin.at[core], pair_send.at[1], pair_recv.at[1], sibling)
    finish.start()

    for i, result in enumerate((out_w, out_m, out_v)):

        def wait_state(d, carry, i=i):
            state_copy(i, d).wait_recv()
            return carry

        lax.fori_loop(1, toks, wait_state, 0)

        def lay_state(p, carry, i=i, result=result):
            both = state[:, i, p].astype(F32)
            result[2 * p] = both[:, :ROWS].reshape(BLOCK, BLOCK).astype(BF16)
            result[2 * p + 1] = both[:, ROWS:].reshape(BLOCK, BLOCK).astype(BF16)
            return carry

        lax.fori_loop(0, half_dev, lay_state, 0)
    finish.wait_recv()
    out_y[...] = fin[...]

    for b in range(2):
        aside(b, 0, 0).wait_send()
        for way in range(2):
            for k in range(steps[b][way]):
                hop(b, way, k).wait_send()
                aside(b, way, k + 1).wait_send()

    def sent_z(d, carry):
        mv_copy(d).wait_send()
        gz_copy(d).wait_send()
        return carry

    def sent_xy(d, carry):
        g_copy(d).wait_send()
        w_copy(d).wait_send()
        for i in range(3):
            state_copy(i, d).wait_send()
        return carry

    lax.fori_loop(1, owners, sent_z, 0)
    lax.fori_loop(1, toks, sent_xy, 0)
    for k in range(to_right):
        rs_copy(0, k).wait_send()
    for k in range(to_left):
        rs_copy(1, k).wait_send()
    swap.wait_send()
    finish.wait_send()


def local(hidden, grad_out, old_weight, old_first, old_second, old_blocks, new_blocks, new_owner):
    owners, toks = lax.axis_size("own"), lax.axis_size("tok")
    chips = owners // 2
    core = lax.axis_index("own") % 2
    per_dev, block = old_weight.shape[0], old_weight.shape[1]
    total = new_owner.shape[0]
    tokens = hidden.shape[0]
    row_share = hidden.shape[1] // block
    width = grad_out.shape[1] * owners
    cols = width // block
    chunk = cols // chips
    half = block // 2
    scale = (total * block * block / width) ** (-0.5)

    lists = jnp.concatenate([new_owner[:, None], old_blocks, new_blocks], axis=1)
    table = pl.pallas_call(
        functools.partial(table_kernel, owners, per_dev, row_share),
        out_shape=jax.ShapeDtypeStruct((TABLE_ROWS, 128), jnp.int32),
        in_specs=[pl.BlockSpec(memory_space=pltpu.VMEM)],
        out_specs=pl.BlockSpec(memory_space=pltpu.VMEM),
        compiler_params=pltpu.CompilerParams(vmem_limit_bytes=32 * 2**20),
        name="block_table",
    )(lists)

    whole = jnp.where(core == 0, grad_out[:, :block], grad_out[:, half:])
    part = jnp.where(core == 0, grad_out[:, block:], grad_out[:, :half])
    cot = jnp.concatenate([whole, jnp.concatenate([part[:half], part[half:]], 1)], 0)

    vmem = pl.BlockSpec(memory_space=pltpu.VMEM)
    hbm = pl.BlockSpec(memory_space=pl.ANY)
    dma = pltpu.SemaphoreType.DMA
    ring = chips // 2
    piece = (chunk, half, block)
    state_shape = jax.ShapeDtypeStruct(old_weight.shape, BF16)
    y, new_weight, new_first, new_second = pl.pallas_call(
        functools.partial(step_kernel, scale),
        out_shape=(jax.ShapeDtypeStruct((2,) + piece, BF16), state_shape, state_shape, state_shape),
        in_specs=[pl.BlockSpec(memory_space=pltpu.SMEM), vmem, vmem, hbm, hbm, hbm],
        out_specs=(vmem, vmem, vmem, vmem),
        scratch_shapes=[
            pltpu.VMEM((3, per_dev, 16, block), BF16),
            pltpu.VMEM((per_dev, 16, block), BF16),
            pltpu.VMEM((owners, 16, block), BF16),
            pltpu.VMEM((owners, 16, block), BF16),
            pltpu.VMEM((owners, block + half, block), BF16),
            pltpu.VMEM((total // 2, 16, block), BF16),
            pltpu.VMEM((cols, tokens, block), BF16),
            pltpu.VMEM((row_share, block, tokens), BF16),
            pltpu.VMEM((toks, owners // 2, 16, block), BF16),
            pltpu.VMEM((toks, owners // 2, 16, block), BF16),
            pltpu.VMEM((owners, ROWS, block), F32),
            pltpu.VMEM((owners, ROWS, block), F32),
            pltpu.VMEM((toks, owners // 2, 16, block), BF16),
            pltpu.VMEM((owners + 1, block, block), BF16),
            pltpu.VMEM((2, cols, half, block), BF16),
            pltpu.VMEM((cols, half, block), BF16),
            pltpu.VMEM((ring,) + piece, BF16),
            pltpu.VMEM((ring,) + piece, BF16),
            pltpu.VMEM((ring,) + piece, BF16),
            pltpu.VMEM((ring,) + piece, BF16),
            pltpu.VMEM((2,) + piece, BF16),
            pltpu.VMEM((toks, 3, per_dev // 2, 16, block), BF16),
            dma((3,)),
            dma((2, 2, ring)),
            dma((2, 2, ring)),
            dma((2, 2, ring + 1)),
            dma((2, 2, ring + 1)),
            dma((2, owners)),
            dma((2, owners)),
            dma((5, toks)),
            dma((5, toks)),
            dma((2, ring)),
            dma((2, ring)),
            dma((2,)),
            dma((2,)),
        ],
        compiler_params=pltpu.CompilerParams(
            collective_id=0, has_side_effects=True, vmem_limit_bytes=48 * 2**20
        ),
        name="projection_step",
    )(table, cot, hidden, old_weight, old_first, old_second)

    y = y.transpose(0, 2, 1, 3).reshape(tokens, chunk * block)
    output = lax.dynamic_slice_in_dim(y, core * grad_out.shape[1], grad_out.shape[1], 1)
    return (output, new_weight, new_first, new_second)


def solution(mesh):
    state = P("own", None, None)
    in_specs = (P("tok", "own"), P("tok", "own"), state, state, state, P(), P(), P())
    out_specs = (P("tok", "own"), state, state, state)
    return jax.shard_map(local, mesh=mesh, in_specs=in_specs, out_specs=out_specs, check_vma=False)
```

time: 479 us -> 131 us (0.27)
  waiting for transfers between devices: 389 us -> 0 us
  Pallas kernels: 0 us -> 122 us
  local copies, waits for them, and re-layouts: 38.2 us -> 7.19 us
  starting transfers between devices: 17.2 us -> 0 us
  between operations: 14 us -> 0.81 us
  matrix products: 8.96 us -> 0 us
  other arithmetic: 8.68 us -> 0.82 us
    all_gather x2 -> x0, waiting for transfers between devices: 187 us -> none  [the longest x1 114 us: local(): gathered = lax.all_gather(hidden, 'own', axis=1, tiled=True)]
    pallas_call x0 -> x2, Pallas kernels: none -> 122 us  [the longest x1 120 us: local(): pl.pallas_call(functools.partial(step_kernel, scale), out_shape=(jax.Shap...]
    reduce_scatter x1 -> x0, waiting for transfers between devices: 102 us -> none  [local(): lax.psum_scatter(partial_value.astype(jnp.bfloat16), 'own', scatter_dimen...]
    psum x1 -> x0, waiting for transfers between devices: 99.1 us -> none  [local(): grad_sum = lax.psum(grad.astype(jnp.bfloat16), 'tok').astype(jnp.float32)]
    all_to_all x1 -> x0, starting transfers between devices: 16.9 us -> none  [local(): lax.all_to_all(outgoing.reshape((owners, capacity) + stacked.shape[1:]),...]
    reshape x3 -> x0, local copies, waits for them, and re-layouts: 11.4 us -> none  [the longest x1 8.63 us: local(): picked = jnp.take(gathered.reshape(tokens, -1, block), rows_new, axis=1)]
    dot_general x5 -> x0, matrix products: 8.96 us -> none  [the longest x1 2.78 us: local(): jnp.einsum('tjk,tjl->jkl', picked, cot_picked, preferred_element_type=jnp...]
    gather x2 -> x0, local copies, waits for them, and re-layouts: 7.29 us -> none  [the longest x1 4.34 us: local(): picked = jnp.take(gathered.reshape(tokens, -1, block), rows_new, axis=1)]
  transfers between devices with their start and end apart: 5 -> 0, of which waited for: 4 -> 0; matrix products, arithmetic and copies ran while one was open for 12% -> 0% of each run, Pallas kernels for 0% -> 0%
where the time goes in v1:
time: 131 us; the launch traced here: 130 us
  Pallas kernels  122 us (93%)
  local copies, waits for them, and re-layouts  7.19 us (5%)
    pallas_call x1, Pallas kernels, local(): pl.pallas_call(functools.partial(step_kernel, scale), out_shape=(jax.Shap...  120 us
    unnamed x19, local copies, waits for them, and re-layouts  6.12 us

profile of v1, /device:TPU:1, one launch (start us, length us, event | category | flops | bytes accessed | tf_op | source)
XLA Modules:
  0.0 130.5 jit_solution(9531360317635541991)
XLA Ops:
  0.6 0.0 copy-start.4
  0.7 0.7 broadcast_in_dim.3
  1.4 0.7 pad_add_fusion
  2.1 0.0 copy-done.4
  2.1 0.0 copy-start
  2.1 0.1 copy.37
  2.2 0.1 copy.36
  2.4 0.1 copy.35
  2.5 0.1 copy.34
  2.7 0.1 maximum_maximum_fusion.cot
  2.7 0.2 copy.27.lists_ref
  2.9 0.0 copy-start.3
  2.9 1.2 block_table.1.table
  4.1 0.0 copy-done
  4.1 0.0 copy-done.3
  4.1 0.0 copy-start.1
  4.1 1.1 copy-done.1
  5.3 0.0 copy-start.2
  5.3 1.1 copy-done.2
  6.4 120.5 %projection_step.1 = (bf16[2,3,64,128]{3,2,1,0:T(8,128)(2,1)S(1)}, bf16[24,128,128]{2,1,0:T(8,128)(2,1)S(1)}, bf16[24,128,128]{2,1,0:T(8,128)(2,1)S(1)}, bf16[24,128,128]{2,1,0:T(8,128)(2,1)S(1)}) custom-call(s32[24,128]{1,0:T(8,128)S(1)} %block_table.1.table, bf16[192,128]{1,0:T(8,128)(2,1)S(1)} %maximum_maximum_fusion.cot, bf16[128,768]{1,0:T(8,128)(2,1)S(1)} %copy-done.3, ...), custom_call_target="tpu_custom_call" | custom-call | tf_op jit(solution)/shard_map/projection_step/pallas_call | solution.py:541
  126.9 0.1 copy.32
  127.0 0.1 constant_dynamic-slice_fusion
  127.1 0.7 copy.33
  127.8 0.9 copy.44
  128.7 0.9 copy.45
  129.6 0.9 copy.46
  (6 shorter events, 0.1 us)
Async XLA Ops:
  0.6 1.4 %copy-start.4 = (bf16[128,192]{0,1:T(8,128)(2,1)S(1)}, bf16[128,192]{0,1:T(8,128)(2,1)}, u32[]{:S(2)}) copy-start(bf16[128,192]{0,1:T(8,128)(2,1)} %param.9) | copy-start | bytes 147460
  2.1 2.0 %copy-start = (bf16[24,128,128]{2,1,0:T(8,128)(2,1)S(1)}, bf16[24,128,128]{2,1,0:T(8,128)(2,1)}, u32[]{:S(2)}) copy-start(bf16[24,128,128]{2,1,0:T(8,128)(2,1)} %old_w.1) | copy-start | bytes 2359300
  2.9 1.2 copy-start.3
  4.1 1.1 copy-start.1
  5.3 1.1 copy-start.2

commit v2 on v0

v2 whole, which is shorter than its diff:
```python
import functools

import jax
import jax.numpy as jnp
from jax import lax
from jax.experimental import pallas as pl
from jax.experimental.pallas import tpu as pltpu
from jax.sharding import PartitionSpec as P

MESH = pl.DeviceIdType.MESH

beta_one = 0.9
beta_two = 0.95
rate = 0.1
epsilon = 0.1
fix_one = 1.0 - 0.9**10
fix_two = 1.0 - 0.95**10

BLOCK = 128
ROWS = 8
F32 = jnp.float32
BF16 = jnp.bfloat16


SEND_SLOT = 0
HOP_OLD, HOP_KEPT = 1, 2
ROW_ROW, ROW_COL = 3, 4
NEW_OLD, NEW_ROW, NEW_KEPT = 5, 6, 7
CELL = 8
TABLE_ROWS = 16


def table_kernel(owners, per_dev, row_share, lists_ref, table_ref):
    me = lax.axis_index("own")
    total = lists_ref.shape[0]
    shape = (total, 128)

    def column(i):
        return jnp.broadcast_to(lists_ref[:, i : i + 1], shape)

    owner, old_row, old_col, new_row, new_col = [column(i) for i in range(5)]
    kept = ((old_row == new_row) & (old_col == new_col)).astype(jnp.int32)
    index = lax.broadcasted_iota(jnp.int32, shape, 0)
    lane = lax.broadcasted_iota(jnp.int32, shape, 1)
    row_in = new_row - me * row_share
    row_mine = (row_in >= 0) & (row_in < row_share)
    zero = jnp.zeros(shape, jnp.int32)

    def pick(where, value):
        return jnp.sum(jnp.where(where, value, zero), axis=0, keepdims=True)

    def put(row, value):
        table_ref[row : row + 1, :] = value

    def place(value, share):
        own = jnp.zeros_like(value)
        for i in range(1, owners):
            own += (value >= i * share).astype(jnp.int32)
        return (own & 1) * (owners // 2) + (own >> 1)

    table_ref[...] = jnp.zeros_like(table_ref)
    local = index - me * per_dev
    put(SEND_SLOT, pick((owner == lane) & (local >= 0) & (local < per_dev), local))

    mine = owner == me
    row_at = new_row - lane * row_share
    hop = pick(mine & (row_at >= 0) & (row_at < row_share), index * 2 + kept)
    put(HOP_OLD, place(hop >> 1, per_dev))
    put(HOP_KEPT, hop & 1)

    at_row = pick((owner == lane) & row_mine, new_col * 256 + row_in)
    put(ROW_COL, at_row >> 8)
    put(ROW_ROW, at_row & 255)

    down = lax.broadcasted_iota(jnp.int32, (total, total), 0)
    across = lax.broadcasted_iota(jnp.int32, (total, total), 1)
    earlier = jnp.where(across < down, 1.0, 0.0).astype(BF16)
    rank = jnp.dot(earlier, jnp.where(mine, 1.0, 0.0).astype(BF16), preferred_element_type=F32)
    at_new = pick(mine & (rank.astype(jnp.int32) == lane), (index * 2 + kept) * 256 + new_row)
    put(NEW_OLD, place(at_new >> 9, per_dev))
    put(NEW_ROW, place(at_new & 255, row_share))
    put(NEW_KEPT, (at_new >> 8) & 1)

    for r in range(row_share):
        put(CELL + r, owners + pick((row_in == r) & (new_col == lane), owner - owners))


def adam_update(weight, first, second, grad):
    moment = beta_one * first + (1.0 - beta_one) * grad
    square = beta_two * second + (1.0 - beta_two) * grad * grad
    change = rate * (moment / fix_one) / (jnp.sqrt(square / fix_two) + epsilon)
    return weight - change, moment, square


JUMP = 5


def step_kernel(
    scale,
    table,
    cot,
    hid,
    old_w,
    old_m,
    old_v,
    out_y,
    out_w,
    out_m,
    out_v,
    loc_w,
    loc_m,
    loc_v,
    w1_out,
    w1_in,
    w2_out,
    w2_in,
    mv_out,
    mv_in,
    cot_all,
    cot_blk,
    hid_b,
    hid_t,
    g_out,
    g_one,
    g_mid,
    g_two,
    g_sum,
    g_new,
    g_all,
    w_all,
    state,
    prod,
    part,
    part_sib,
    rs_out,
    rs_in,
    fin,
    loc_sem,
    cot_send,
    cot_recv,
    sib_send,
    sib_recv,
    z_send,
    z_recv,
    fwd_send,
    fwd_recv,
    xy_send,
    xy_recv,
    rs_send,
    rs_recv,
):
    toks, owners = lax.axis_size("tok"), lax.axis_size("own")
    side = 4
    chips = owners // 2
    t, o = lax.axis_index("tok"), lax.axis_index("own")
    z, core = o // 2, o % 2
    y, x = t // side, t % side
    sibling = {"tok": t, "own": z * 2 + 1 - core}
    per_dev = old_w.shape[0]
    half_dev = per_dev // 2
    row_share = hid_t.shape[0]
    cols = cot_blk.shape[0]
    chunk = cols // chips
    half = BLOCK // 2
    pairs = owners // 2
    reach = (chips // 2, chips - 1 - chips // 2)

    def remote(src, dst, send, recv, device):
        return pltpu.make_async_remote_copy(
            src_ref=src, dst_ref=dst, send_sem=send, recv_sem=recv, device_id=device, device_id_type=MESH
        )

    def along_z(d):
        return {"tok": t, "own": ((z + d) % chips) * 2 + core}

    def tok_at(dy, dx):
        return ((y + dy) % side) * side + (x + dx) % side

    def across(dy, dx):
        return {"tok": tok_at(dy, dx), "own": o}

    def loop(first, last, body):
        def step(i, carry):
            body(i)
            return carry

        lax.fori_loop(first, last, step, 0)

    loc = (loc_w, loc_m, loc_v)

    rows = pl.ds((t // 2) * 16, 16)
    local = [
        pltpu.make_async_copy(old.at[:, rows, :], loc[i], loc_sem.at[i])
        for i, old in enumerate((old_w, old_m, old_v))
    ]
    for copy in local:
        copy.start()
    barrier = pltpu.get_barrier_semaphore()

    def greet(device):
        pl.semaphore_signal(barrier, inc=1, device_id=device, device_id_type=MESH)

    greet(sibling)
    loop(1, chips, lambda d: greet(along_z(d)))
    loop(1, side, lambda d: greet(across(0, d)))
    loop(1, side, lambda d: greet(across(d, 0)))

    def is_one(bit):
        return (jnp.zeros((ROWS, BLOCK), jnp.int32) + bit) == 1

    odd_rows, second_core = is_one(t % 2), is_one(core)

    def own_rows(i, k):
        both = loc[i][k].astype(F32)
        return jnp.where(odd_rows, both[ROWS:], both[:ROWS])

    def core_rows(tile):
        both = tile.astype(F32)
        return jnp.where(second_core, both[ROWS:], both[:ROWS])

    def stack(a, b):
        return jnp.concatenate([a, b], 0).astype(BF16)

    cot_all[o] = cot[...]
    local[0].wait()

    def pack_w1(k):
        w1_out[k] = stack(own_rows(0, table[SEND_SLOT, 2 * k]), own_rows(0, table[SEND_SLOT, 2 * k + 1]))

    loop(0, chips, pack_w1)
    pl.semaphore_wait(barrier, chips - 1 + 1 + 2 * (side - 1))

    def cot_at(way, distance):
        zz = z + chips - distance if way == 0 else z + distance
        return cot_all.at[(zz % chips) * 2 + core]

    def cot_hop(way, distance):
        step = distance if distance in (1, JUMP) else 1
        ref = cot_at(way, distance - step)
        return remote(
            ref,
            ref,
            cot_send.at[way, distance],
            cot_recv.at[way, distance],
            along_z(step if way == 0 else chips - step),
        )

    def cot_aside(way, distance):
        ref = cot_at(way, distance)
        return remote(ref, ref, sib_send.at[way, distance], sib_recv.at[way, distance], sibling)

    def cot_step(distance):
        for way in range(2):
            if distance <= reach[way]:
                cot_hop(way, distance).wait_recv()
                if distance + 1 <= reach[way] and distance + 1 != JUMP:
                    cot_hop(way, distance + 1).start()
                cot_aside(way, distance).start()

    def far_first(i):
        return chips // 2 + ((i + 1) // 2) * (1 - 2 * (i % 2))

    def z_copy(plane, src, dst, d):
        zz = (z + d) % chips
        return remote(
            src(zz),
            dst.at[core * chips + z],
            z_send.at[plane, d],
            z_recv.at[plane, d],
            {"tok": t, "own": zz * 2 + core},
        )

    def forward(plane, ref):
        return remote(ref, ref, fwd_send.at[plane], fwd_recv.at[plane], sibling)

    my_chips = pl.ds(core * chips, chips)
    z_all = {
        "w1": (0, lambda zz: w1_out.at[zz], w1_in),
        "mv": (1, lambda zz: mv_out.at[pl.ds(2 * zz, 2)], mv_in),
        "w2": (2, lambda zz: w2_out.at[zz], w2_in),
        "g": (3, lambda zz: g_sum.at[zz], g_new),
    }
    fwd = {
        "w1": forward(0, w1_in.at[my_chips]),
        "mv": forward(1, mv_in.at[my_chips, 1 - core]),
        "w2": forward(2, w2_in.at[my_chips]),
        "g": forward(3, g_new.at[my_chips]),
    }

    def z_start(name):
        loop(0, chips - 1, lambda i: z_copy(*z_all[name], far_first(i)).start())

    def z_wait(name):
        loop(1, chips, lambda d: z_copy(*z_all[name], d).wait_recv())
        fwd[name].start()

    def xy_one(plane, at, h, d):
        ref = at(h, t)
        to = across(0, d) if h == 0 else across(d, 0)
        return remote(ref, ref, xy_send.at[plane, h, 0, d], xy_recv.at[plane, h, 0, d], to)

    def xy_two(plane, at, h, e, d):
        ref = at(h, tok_at(0, e) if h == 0 else tok_at(e, 0))
        to = across(d, 0) if h == 0 else across(0, d)
        return remote(ref, ref, xy_send.at[plane, h, 1 + e, d], xy_recv.at[plane, h, 1 + e, d], to)

    def ag_start(plane, at):
        for h in range(2):
            loop(1, side, lambda d: xy_one(plane, at, h, d).start())
        for h in range(2):
            loop(1, side, lambda d: xy_two(plane, at, h, 0, d).start())

    def ag_pass_on(plane, at):
        def pass_on(d):
            for h in range(2):
                xy_one(plane, at, h, d).wait_recv()
                loop(1, side, lambda dd: xy_two(plane, at, h, side - d, dd).start())

        loop(1, side, pass_on)

    def ag_each(plane, at, do):
        for h in range(2):
            loop(0, side, lambda e: loop(1, side, lambda d: do(xy_two(plane, at, h, e, d))))

    def ag_wait(plane, at):
        ag_each(plane, at, lambda copy: copy.wait_recv())

    def ag_sent(plane, at):
        for h in range(2):
            loop(1, side, lambda d: xy_one(plane, at, h, d).wait_send())
        ag_each(plane, at, lambda copy: copy.wait_send())

    def halves(ref):
        n = ref.shape[1] // 2
        return lambda h, i: ref.at[i, pl.ds(h * n, n)]

    ag_w, ag_state, ag_g = (0, halves(w_all)), (1, halves(state)), (2, halves(g_all))

    for way in range(2):
        cot_hop(way, 1).start()
    for way in range(2):
        if JUMP <= reach[way]:
            cot_hop(way, JUMP).start()
    z_start("w1")
    cot_aside(0, 0).start()
    w1_in[core * chips + z] = w1_out[z]

    for i in (1, 2):
        local[i].wait()

    def pack_mv(n):
        k = table[SEND_SLOT, n]
        mv_out[n] = stack(own_rows(1, k), own_rows(2, k))

    loop(0, owners, pack_mv)
    z_start("mv")
    mv_in[core * chips + z] = mv_out[pl.ds(2 * z, 2)]

    for r in range(row_share):
        block = hid[:, r * BLOCK : (r + 1) * BLOCK]
        hid_b[r] = block
        hid_t[r] = block.astype(F32).T.astype(BF16)
    prod[owners] = jnp.zeros(prod.shape[1:], F32)

    for distance in (1, 5, 2, 6):
        cot_step(distance)
    z_wait("w1")
    cot_step(3)
    fwd["w1"].wait_recv()

    def pack_w2(k):
        parts = []
        for r in (2 * k, 2 * k + 1):
            parts.append(core_rows(w1_in[table[HOP_OLD, r]]) * table[HOP_KEPT, r].astype(F32))
        w2_out[k] = stack(*parts)

    loop(0, chips, pack_w2)
    z_start("w2")
    w2_in[core * chips + z] = w2_out[z]
    for distance in (7, 4, 8):
        cot_step(distance)
    z_wait("mv")

    cot_aside(0, 0).wait_recv()
    for way in range(2):
        for distance in range(1, reach[way] + 1):
            cot_aside(way, distance).wait_recv()

    low = lax.broadcasted_iota(jnp.int32, (half, BLOCK), 1) < half

    def lay_cot(zz):
        first, last = cot_all[2 * zz], cot_all[2 * zz + 1]
        cot_blk[3 * zz] = first[:BLOCK]
        cot_blk[3 * zz + 2] = last[:BLOCK]
        a, b = first[BLOCK:].astype(F32), last[BLOCK:].astype(F32)
        top = jnp.where(low, a, pltpu.roll(b, half, 1))
        bottom = jnp.where(low, pltpu.roll(a, half, 1), b)
        cot_blk[3 * zz + 1] = stack(top, bottom)

    loop(0, chips, lay_cot)

    def grad_pair(k):
        slices = []
        for n in (2 * k, 2 * k + 1):
            g = jnp.dot(hid_t[table[ROW_ROW, n]], cot_blk[table[ROW_COL, n]], preferred_element_type=F32)
            slices.append((g * scale).reshape(toks, ROWS, BLOCK))
        g_out[:, k] = jnp.concatenate(slices, 1).astype(BF16)

    loop(0, pairs, grad_pair)

    def half_pairs(h):
        return pl.ds(h * (pairs // 2), pairs // 2)

    def g_first(h, e, d):
        to = tok_at(e, d) if h == 0 else tok_at(d, e)
        return remote(
            g_out.at[to, half_pairs(h)],
            g_one.at[h, d, e],
            xy_send.at[3, h, 1 + e, d],
            xy_recv.at[3, h, 1 + e, d],
            across(0, d) if h == 0 else across(d, 0),
        )

    def g_second(h, e):
        return remote(
            g_mid.at[h, e],
            g_two.at[h, e],
            xy_send.at[3, h, 0, e],
            xy_recv.at[3, h, 0, e],
            across(e, 0) if h == 0 else across(0, e),
        )

    def g_each(do):
        for h in range(2):
            loop(1, side, lambda e: loop(1, side, lambda d: do(g_first(h, e, d))))
        for h in range(2):
            loop(1, side, lambda d: do(g_first(h, 0, d)))

    g_each(lambda copy: copy.start())

    fwd["mv"].wait_recv()

    def pack_state(p):
        parts = []
        for s in (2 * p, 2 * p + 1):
            kept = table[NEW_KEPT, s].astype(F32)
            place = table[NEW_OLD, s]
            both = mv_in[place, core].astype(F32) * kept
            parts.append((core_rows(w1_in[place]) * kept, both[:ROWS], both[ROWS:]))
        for i in range(3):
            state[t, i * half_dev + p] = stack(parts[0][i], parts[1][i])

    loop(0, half_dev, pack_state)

    z_wait("w2")
    fwd["w2"].wait_recv()

    def pack_w(k):
        w_all[t, k] = stack(core_rows(w2_in[k]), core_rows(w2_in[chips + k]))

    loop(0, pairs, pack_w)
    ag_start(*ag_w)
    ag_pass_on(*ag_w)
    ag_start(*ag_state)

    def g_middle(e):
        for h in range(2):
            loop(1, side, lambda d: g_first(h, e, d).wait_recv())
            own = g_out[tok_at(e, 0) if h == 0 else tok_at(0, e), half_pairs(h)].astype(F32)
            others = [g_one[h, d, e].astype(F32) for d in range(1, side)]
            g_mid[h, e] = (own + others[0] + others[1] + others[2]).astype(BF16)

    def g_on(e):
        g_middle(e)
        for h in range(2):
            g_second(h, e).start()

    loop(1, side, g_on)
    g_middle(0)
    for h in range(2):
        loop(1, side, lambda e: g_second(h, e).wait_recv())
        total = g_mid[h, 0].astype(F32)
        for e in range(1, side):
            total += g_two[h, e].astype(F32)
        g_sum[half_pairs(h)] = total.astype(BF16)
    z_start("g")
    g_new[core * chips + z] = g_sum[z]
    ag_pass_on(*ag_state)

    ag_wait(*ag_w)

    def product(k):
        both = w_all[:, k].astype(F32)
        for i in range(2):
            n = 2 * k + i
            w = both[:, i * ROWS : (i + 1) * ROWS].reshape(BLOCK, BLOCK).astype(BF16)
            p = jnp.dot(hid_b[table[ROW_ROW, n]], w, preferred_element_type=F32) * scale
            prod[n] = p.reshape(2, half, BLOCK)

    loop(0, pairs, product)

    def gather_part(h):
        def column(c):
            total = prod[table[CELL, c], h]
            for r in range(1, row_share):
                total += prod[table[CELL + r, c], h]
            part[h, c] = total.astype(BF16)

        loop(0, cols, column)

    gather_part(1 - core)
    swap = remote(part.at[1 - core], part_sib, fwd_send.at[4], fwd_recv.at[4], sibling)
    swap.start()
    gather_part(core)
    swap.wait_recv()

    def term(zz):
        at = pl.ds((zz % chips) * chunk, chunk)
        return part[core, at].astype(F32) + part_sib[at].astype(F32)

    def rs_hop(way, distance):
        step = JUMP if distance == JUMP else 1
        return remote(
            rs_out.at[way, distance],
            rs_in.at[way, distance],
            rs_send.at[way, distance],
            rs_recv.at[way, distance],
            along_z(step if way == 0 else chips - step),
        )

    def rs_step(way, distance):
        if distance > reach[way]:
            return
        value = term(z + distance if way == 0 else z + chips - distance)
        if distance not in (JUMP - 1, reach[way]):
            rs_hop(way, distance + 1).wait_recv()
            value += rs_in[way, distance + 1].astype(F32)
        rs_out[way, distance] = value.astype(BF16)
        rs_hop(way, distance).start()

    def rs_round(k):
        for way in range(2):
            if reach[way] - k >= JUMP:
                rs_step(way, reach[way] - k)
        for way in range(2):
            if JUMP - 1 - k >= 1:
                rs_step(way, min(JUMP - 1, reach[way]) - k)

    rs_round(0)

    z_wait("g")
    fwd["g"].wait_recv()

    def pack_g(p):
        g_all[t, p] = stack(*[core_rows(g_new[table[NEW_ROW, s]]) for s in (2 * p, 2 * p + 1)])

    loop(0, half_dev, pack_g)
    ag_start(*ag_g)
    rs_round(1)
    ag_pass_on(*ag_g)
    rs_round(2)
    rs_round(3)

    ag_wait(*ag_state)
    ag_wait(*ag_g)

    def adam(p):
        g, w, m, v = [
            ref[:, i].astype(F32)
            for ref, i in ((g_all, p), (state, p), (state, half_dev + p), (state, 2 * half_dev + p))
        ]
        for result, value in zip((out_w, out_m, out_v), adam_update(w, m, v, g)):
            for i in range(2):
                part_rows = value[:, i * ROWS : (i + 1) * ROWS]
                result[2 * p + i] = part_rows.reshape(BLOCK, BLOCK).astype(BF16)

    loop(0, half_dev, adam)

    value = term(z)
    for way in range(2):
        for distance in (1, JUMP):
            if distance <= reach[way]:
                rs_hop(way, distance).wait_recv()
                value += rs_in[way, distance].astype(F32)
    fin[core] = value.astype(BF16)
    finish = remote(fin.at[core], fin.at[core], fwd_send.at[5], fwd_recv.at[5], sibling)
    finish.start()
    finish.wait_recv()
    out_y[...] = fin[...]

    cot_aside(0, 0).wait_send()
    for way in range(2):
        for distance in range(1, reach[way] + 1):
            cot_hop(way, distance).wait_send()
            cot_aside(way, distance).wait_send()
            rs_hop(way, distance).wait_send()
    for name in z_all:
        loop(1, chips, lambda d: z_copy(*z_all[name], d).wait_send())
        fwd[name].wait_send()
    for gather in (ag_w, ag_state, ag_g):
        ag_sent(*gather)
    g_each(lambda copy: copy.wait_send())
    for h in range(2):
        loop(1, side, lambda e: g_second(h, e).wait_send())
    swap.wait_send()
    finish.wait_send()


def local(hidden, grad_out, old_weight, old_first, old_second, old_blocks, new_blocks, new_owner):
    owners, toks = lax.axis_size("own"), lax.axis_size("tok")
    chips = owners // 2
    core = lax.axis_index("own") % 2
    per_dev, block = old_weight.shape[0], old_weight.shape[1]
    total = new_owner.shape[0]
    tokens = hidden.shape[0]
    row_share = hidden.shape[1] // block
    width = grad_out.shape[1] * owners
    cols = width // block
    chunk = cols // chips
    half = block // 2
    scale = (total * block * block / width) ** (-0.5)

    lists = jnp.concatenate([new_owner[:, None], old_blocks, new_blocks], axis=1)
    table = pl.pallas_call(
        functools.partial(table_kernel, owners, per_dev, row_share),
        out_shape=jax.ShapeDtypeStruct((TABLE_ROWS, 128), jnp.int32),
        in_specs=[pl.BlockSpec(memory_space=pltpu.VMEM)],
        out_specs=pl.BlockSpec(memory_space=pltpu.VMEM),
        compiler_params=pltpu.CompilerParams(vmem_limit_bytes=32 * 2**20),
        name="block_table",
    )(lists)

    whole = jnp.where(core == 0, grad_out[:, :block], grad_out[:, half:])
    part = jnp.where(core == 0, grad_out[:, block:], grad_out[:, :half])
    cot = jnp.concatenate([whole, jnp.concatenate([part[:half], part[half:]], 1)], 0)

    vmem = pl.BlockSpec(memory_space=pltpu.VMEM)
    hbm = pl.BlockSpec(memory_space=pl.ANY)
    dma = pltpu.SemaphoreType.DMA
    ring = chips // 2
    piece = (chunk, half, block)
    state_shape = jax.ShapeDtypeStruct(old_weight.shape, BF16)
    y, new_weight, new_first, new_second = pl.pallas_call(
        functools.partial(step_kernel, scale),
        out_shape=(jax.ShapeDtypeStruct((2,) + piece, BF16), state_shape, state_shape, state_shape),
        in_specs=[pl.BlockSpec(memory_space=pltpu.SMEM), vmem, vmem, hbm, hbm, hbm],
        out_specs=(vmem, vmem, vmem, vmem),
        scratch_shapes=[
            pltpu.VMEM((per_dev, 16, block), BF16),
            pltpu.VMEM((per_dev, 16, block), BF16),
            pltpu.VMEM((per_dev, 16, block), BF16),
            pltpu.VMEM((chips, 16, block), BF16),
            pltpu.VMEM((owners, 16, block), BF16),
            pltpu.VMEM((chips, 16, block), BF16),
            pltpu.VMEM((owners, 16, block), BF16),
            pltpu.VMEM((owners, 16, block), BF16),
            pltpu.VMEM((owners, 2, 16, block), BF16),
            pltpu.VMEM((owners, block + half, block), BF16),
            pltpu.VMEM((cols, tokens, block), BF16),
            pltpu.VMEM((row_share, tokens, block), BF16),
            pltpu.VMEM((row_share, block, tokens), BF16),
            pltpu.VMEM((toks, chips, 16, block), BF16),
            pltpu.VMEM((2, 4, 4, chips // 2, 16, block), BF16),
            pltpu.VMEM((2, 4, chips // 2, 16, block), BF16),
            pltpu.VMEM((2, 4, chips // 2, 16, block), BF16),
            pltpu.VMEM((chips, 16, block), BF16),
            pltpu.VMEM((owners, 16, block), BF16),
            pltpu.VMEM((toks, per_dev // 2, 16, block), BF16),
            pltpu.VMEM((toks, chips, 16, block), BF16),
            pltpu.VMEM((toks, 3 * per_dev // 2, 16, block), BF16),
            pltpu.VMEM((owners + 1, 2, half, block), F32),
            pltpu.VMEM((2, cols, half, block), BF16),
            pltpu.VMEM((cols, half, block), BF16),
            pltpu.VMEM((2, ring + 1) + piece, BF16),
            pltpu.VMEM((2, ring + 1) + piece, BF16),
            pltpu.VMEM((2,) + piece, BF16),
            dma((3,)),
            dma((2, ring + 1)),
            dma((2, ring + 1)),
            dma((2, ring + 1)),
            dma((2, ring + 1)),
            dma((4, chips)),
            dma((4, chips)),
            dma((6,)),
            dma((6,)),
            dma((4, 2, 5, 4)),
            dma((4, 2, 5, 4)),
            dma((2, ring + 1)),
            dma((2, ring + 1)),
        ],
        compiler_params=pltpu.CompilerParams(
            collective_id=0, has_side_effects=True, vmem_limit_bytes=48 * 2**20
        ),
        name="projection_step",
    )(table, cot, hidden, old_weight, old_first, old_second)

    y = y.transpose(0, 2, 1, 3).reshape(tokens, chunk * block)
    output = lax.dynamic_slice_in_dim(y, core * grad_out.shape[1], grad_out.shape[1], 1)
    return (output, new_weight, new_first, new_second)


def solution(mesh):
    state = P("own", None, None)
    in_specs = (P("tok", "own"), P("tok", "own"), state, state, state, P(), P(), P())
    out_specs = (P("tok", "own"), state, state, state)
    return jax.shard_map(local, mesh=mesh, in_specs=in_specs, out_specs=out_specs, check_vma=False)
```

time: 479 us -> 118 us (0.25)
  waiting for transfers between devices: 389 us -> 0 us
  Pallas kernels: 0 us -> 109 us
  local copies, waits for them, and re-layouts: 38.2 us -> 7.19 us
  starting transfers between devices: 17.2 us -> 0 us
  between operations: 14 us -> 0.81 us
  matrix products: 8.96 us -> 0 us
  other arithmetic: 8.68 us -> 0.82 us
    all_gather x2 -> x0, waiting for transfers between devices: 187 us -> none  [the longest x1 114 us: local(): gathered = lax.all_gather(hidden, 'own', axis=1, tiled=True)]
    pallas_call x0 -> x2, Pallas kernels: none -> 109 us  [the longest x1 107 us: local(): pl.pallas_call(functools.partial(step_kernel, scale), out_shape=(jax.Shap...]
    reduce_scatter x1 -> x0, waiting for transfers between devices: 102 us -> none  [local(): lax.psum_scatter(partial_value.astype(jnp.bfloat16), 'own', scatter_dimen...]
    psum x1 -> x0, waiting for transfers between devices: 99.1 us -> none  [local(): grad_sum = lax.psum(grad.astype(jnp.bfloat16), 'tok').astype(jnp.float32)]
    all_to_all x1 -> x0, starting transfers between devices: 16.9 us -> none  [local(): lax.all_to_all(outgoing.reshape((owners, capacity) + stacked.shape[1:]),...]
    reshape x3 -> x0, local copies, waits for them, and re-layouts: 11.4 us -> none  [the longest x1 8.63 us: local(): picked = jnp.take(gathered.reshape(tokens, -1, block), rows_new, axis=1)]
    dot_general x5 -> x0, matrix products: 8.96 us -> none  [the longest x1 2.78 us: local(): jnp.einsum('tjk,tjl->jkl', picked, cot_picked, preferred_element_type=jnp...]
    gather x2 -> x0, local copies, waits for them, and re-layouts: 7.29 us -> none  [the longest x1 4.34 us: local(): picked = jnp.take(gathered.reshape(tokens, -1, block), rows_new, axis=1)]
  transfers between devices with their start and end apart: 5 -> 0, of which waited for: 4 -> 0; matrix products, arithmetic and copies ran while one was open for 12% -> 0% of each run, Pallas kernels for 0% -> 0%
where the time goes in v2:
time: 118 us; the launch traced here: 117 us
  Pallas kernels  109 us (92%)
  local copies, waits for them, and re-layouts  7.19 us (6%)
    pallas_call x1, Pallas kernels, local(): pl.pallas_call(functools.partial(step_kernel, scale), out_shape=(jax.Shap...  107 us
    unnamed x19, local copies, waits for them, and re-layouts  6.12 us

profile of v2, /device:TPU:1, one launch (start us, length us, event | category | flops | bytes accessed | tf_op | source)
XLA Modules:
  0.0 117.4 jit_solution(1444926115794837888)
XLA Ops:
  0.6 0.0 copy-start.4
  0.7 0.7 broadcast_in_dim.3
  1.4 0.7 pad_add_fusion
  2.1 0.0 copy-done.4
  2.1 0.0 copy-start
  2.1 0.1 copy.37
  2.2 0.1 copy.36
  2.4 0.1 copy.35
  2.5 0.1 copy.34
  2.7 0.1 maximum_maximum_fusion.cot
  2.7 0.2 copy.27.lists_ref
  2.9 0.0 copy-start.3
  2.9 1.2 %block_table.1.table = s32[16,128]{1,0:T(8,128)S(1)} custom-call(s32[768,5]{1,0:T(8,128)S(1)} %copy.27.lists_ref), custom_call_target="tpu_custom_call" | custom-call | tf_op jit(solution)/shard_map/block_table/pallas_call | solution.py:624
  4.2 0.0 copy-done
  4.2 0.0 copy-done.3
  4.2 0.0 copy-start.1
  4.2 1.1 copy-done.1
  5.3 0.0 copy-start.2
  5.3 1.1 copy-done.2
  6.5 107.3 %projection_step.1 = (bf16[2,3,64,128]{3,2,1,0:T(8,128)(2,1)S(1)}, bf16[24,128,128]{2,1,0:T(8,128)(2,1)S(1)}, bf16[24,128,128]{2,1,0:T(8,128)(2,1)S(1)}, bf16[24,128,128]{2,1,0:T(8,128)(2,1)S(1)}) custom-call(s32[16,128]{1,0:T(8,128)S(1)} %block_table.1.table, bf16[192,128]{1,0:T(8,128)(2,1)S(1)} %maximum_maximum_fusion.cot, bf16[128,768]{1,0:T(8,128)(2,1)S(1)} %copy-done.3, ...), custom_call_target="tpu_custom_call" | custom-call | tf_op jit(solution)/shard_map/projection_step/pallas_call | solution.py:643
  113.8 0.1 copy.32
  113.9 0.1 constant_dynamic-slice_fusion
  114.0 0.7 copy.33
  114.8 0.9 copy.44
  115.6 0.9 copy.45
  116.5 0.9 copy.46
  (6 shorter events, 0.1 us)
Async XLA Ops:
  0.6 1.4 %copy-start.4 = (bf16[128,192]{0,1:T(8,128)(2,1)S(1)}, bf16[128,192]{0,1:T(8,128)(2,1)}, u32[]{:S(2)}) copy-start(bf16[128,192]{0,1:T(8,128)(2,1)} %param.9) | copy-start | bytes 147460
  2.1 2.1 %copy-start = (bf16[24,128,128]{2,1,0:T(8,128)(2,1)S(1)}, bf16[24,128,128]{2,1,0:T(8,128)(2,1)}, u32[]{:S(2)}) copy-start(bf16[24,128,128]{2,1,0:T(8,128)(2,1)} %old_w.1) | copy-start | bytes 2359300
  2.9 1.3 %copy-start.3 = (bf16[128,768]{1,0:T(8,128)(2,1)S(1)}, bf16[128,768]{1,0:T(8,128)(2,1)}, u32[]{:S(2)}) copy-start(bf16[128,768]{1,0:T(8,128)(2,1)} %hid.1) | copy-start | bytes 589828
  4.2 1.1 copy-start.1
  5.3 1.1 copy-start.2

commit v3 on v2

--- a/solution.py
+++ b/solution.py
@@ -30,27 +30,31 @@
 TABLE_ROWS = 16
 
 
-def table_kernel(owners, per_dev, row_share, lists_ref, table_ref):
+def table_kernel(owners, per_dev, row_share, cols, owner_ref, old_ref, new_ref, table_ref):
     me = lax.axis_index("own")
-    total = lists_ref.shape[0]
-    shape = (total, 128)
-
-    def column(i):
-        return jnp.broadcast_to(lists_ref[:, i : i + 1], shape)
-
-    owner, old_row, old_col, new_row, new_col = [column(i) for i in range(5)]
-    kept = ((old_row == new_row) & (old_col == new_col)).astype(jnp.int32)
-    index = lax.broadcasted_iota(jnp.int32, shape, 0)
-    lane = lax.broadcasted_iota(jnp.int32, shape, 1)
+    total = owner_ref.shape[0]
+    shape = (cols, total)
+
+    def spread(row):
+        return jnp.broadcast_to(row, shape)
+
+    owner = spread(owner_ref[...].reshape(1, total))
+    new_row, new_col = spread(new_ref[0:1, :]), spread(new_ref[1:2, :])
+    same = (old_ref[0:1, :] == new_ref[0:1, :]) & (old_ref[1:2, :] == new_ref[1:2, :])
+    kept = spread(same.astype(jnp.int32))
+    slot = lax.broadcasted_iota(jnp.int32, shape, 0)
+    index = lax.broadcasted_iota(jnp.int32, shape, 1)
     row_in = new_row - me * row_share
     row_mine = (row_in >= 0) & (row_in < row_share)
     zero = jnp.zeros(shape, jnp.int32)
+    lane = lax.broadcasted_iota(jnp.int32, (cols, 128), 1)
+    columns = []
 
     def pick(where, value):
-        return jnp.sum(jnp.where(where, value, zero), axis=0, keepdims=True)
+        return jnp.sum(jnp.where(where, value, zero), axis=1, keepdims=True)
 
     def put(row, value):
-        table_ref[row : row + 1, :] = value
+        columns.append((row, value))
 
     def place(value, share):
         own = jnp.zeros_like(value)
@@ -58,37 +62,43 @@
             own += (value >= i * share).astype(jnp.int32)
         return (own & 1) * (owners // 2) + (own >> 1)
 
-    table_ref[...] = jnp.zeros_like(table_ref)
     local = index - me * per_dev
-    put(SEND_SLOT, pick((owner == lane) & (local >= 0) & (local < per_dev), local))
+    put(SEND_SLOT, pick((owner == slot) & (local >= 0) & (local < per_dev), local))
 
     mine = owner == me
-    row_at = new_row - lane * row_share
+    row_at = new_row - slot * row_share
     hop = pick(mine & (row_at >= 0) & (row_at < row_share), index * 2 + kept)
     put(HOP_OLD, place(hop >> 1, per_dev))
     put(HOP_KEPT, hop & 1)
 
-    at_row = pick((owner == lane) & row_mine, new_col * 256 + row_in)
+    at_row = pick((owner == slot) & row_mine, new_col * 256 + row_in)
     put(ROW_COL, at_row >> 8)
     put(ROW_ROW, at_row & 255)
 
     down = lax.broadcasted_iota(jnp.int32, (total, total), 0)
     across = lax.broadcasted_iota(jnp.int32, (total, total), 1)
-    earlier = jnp.where(across < down, 1.0, 0.0).astype(BF16)
-    rank = jnp.dot(earlier, jnp.where(mine, 1.0, 0.0).astype(BF16), preferred_element_type=F32)
-    at_new = pick(mine & (rank.astype(jnp.int32) == lane), (index * 2 + kept) * 256 + new_row)
+    earlier = jnp.where(down < across, 1.0, 0.0).astype(BF16)
+    mine_once = jnp.where(mine[:16], 1.0, 0.0).astype(BF16)
+    rank = jnp.dot(mine_once, earlier, preferred_element_type=F32)[0:1, :].astype(jnp.int32)
+    at_new = pick(mine & (spread(rank) == slot), (index * 2 + kept) * 256 + new_row)
     put(NEW_OLD, place(at_new >> 9, per_dev))
     put(NEW_ROW, place(at_new & 255, row_share))
     put(NEW_KEPT, (at_new >> 8) & 1)
 
     for r in range(row_share):
-        put(CELL + r, owners + pick((row_in == r) & (new_col == lane), owner - owners))
+        put(CELL + r, owners + pick((row_in == r) & (new_col == slot), owner - owners))
+
+    turned = jnp.zeros((cols, 128), F32)
+    for row, value in columns:
+        turned = jnp.where(lane == row, value.astype(F32), turned)
+    turned = jnp.concatenate([turned, jnp.zeros((128 - cols, 128), F32)], 0).T
+    table_ref[...] = turned[:TABLE_ROWS].astype(jnp.int32)
 
 
 def adam_update(weight, first, second, grad):
     moment = beta_one * first + (1.0 - beta_one) * grad
     square = beta_two * second + (1.0 - beta_two) * grad * grad
-    change = rate * (moment / fix_one) / (jnp.sqrt(square / fix_two) + epsilon)
+    change = (rate / fix_one) * moment / (jnp.sqrt(square * (1.0 / fix_two)) + epsilon)
     return weight - change, moment, square
 
 
@@ -117,7 +127,6 @@
     mv_out,
     mv_in,
     cot_all,
-    cot_blk,
     hid_b,
     hid_t,
     g_out,
@@ -159,7 +168,8 @@
     per_dev = old_w.shape[0]
     half_dev = per_dev // 2
     row_share = hid_t.shape[0]
-    cols = cot_blk.shape[0]
+    cols = part.shape[1]
+    units = cot.shape[0] // (BLOCK // 2)
     chunk = cols // chips
     half = BLOCK // 2
     pairs = owners // 2
@@ -187,6 +197,13 @@
         lax.fori_loop(first, last, step, 0)
 
     loc = (loc_w, loc_m, loc_v)
+
+    def loop_by(n, last, body):
+        def several(i):
+            for j in range(n):
+                body(i * n + j)
+
+        loop(0, last // n, several)
 
     rows = pl.ds((t // 2) * 16, 16)
     local = [
@@ -221,18 +238,20 @@
     def stack(a, b):
         return jnp.concatenate([a, b], 0).astype(BF16)
 
-    cot_all[o] = cot[...]
+    for i in range(units):
+        cot_all[o * units + i] = cot[i * half : (i + 1) * half, :]
     local[0].wait()
 
     def pack_w1(k):
         w1_out[k] = stack(own_rows(0, table[SEND_SLOT, 2 * k]), own_rows(0, table[SEND_SLOT, 2 * k + 1]))
 
-    loop(0, chips, pack_w1)
+    loop_by(4, chips, pack_w1)
     pl.semaphore_wait(barrier, chips - 1 + 1 + 2 * (side - 1))
 
     def cot_at(way, distance):
         zz = z + chips - distance if way == 0 else z + distance
-        return cot_all.at[(zz % chips) * 2 + core]
+        own = (zz % chips) * 2 + core
+        return cot_all.at[pl.ds(own * units, units)]
 
     def cot_hop(way, distance):
         step = distance if distance in (1, JUMP) else 1
@@ -336,77 +355,63 @@
 
     ag_w, ag_state, ag_g = (0, halves(w_all)), (1, halves(state)), (2, halves(g_all))
 
-    for way in range(2):
-        cot_hop(way, 1).start()
-    for way in range(2):
-        if JUMP <= reach[way]:
-            cot_hop(way, JUMP).start()
-    z_start("w1")
-    cot_aside(0, 0).start()
-    w1_in[core * chips + z] = w1_out[z]
-
-    for i in (1, 2):
-        local[i].wait()
-
-    def pack_mv(n):
-        k = table[SEND_SLOT, n]
-        mv_out[n] = stack(own_rows(1, k), own_rows(2, k))
-
-    loop(0, owners, pack_mv)
-    z_start("mv")
-    mv_in[core * chips + z] = mv_out[pl.ds(2 * z, 2)]
-
-    for r in range(row_share):
-        block = hid[:, r * BLOCK : (r + 1) * BLOCK]
-        hid_b[r] = block
-        hid_t[r] = block.astype(F32).T.astype(BF16)
-    prod[owners] = jnp.zeros(prod.shape[1:], F32)
-
-    for distance in (1, 5, 2, 6):
-        cot_step(distance)
-    z_wait("w1")
-    cot_step(3)
-    fwd["w1"].wait_recv()
-
-    def pack_w2(k):
-        parts = []
-        for r in (2 * k, 2 * k + 1):
-            parts.append(core_rows(w1_in[table[HOP_OLD, r]]) * table[HOP_KEPT, r].astype(F32))
-        w2_out[k] = stack(*parts)
-
-    loop(0, chips, pack_w2)
-    z_start("w2")
-    w2_in[core * chips + z] = w2_out[z]
-    for distance in (7, 4, 8):
-        cot_step(distance)
-    z_wait("mv")
-
-    cot_aside(0, 0).wait_recv()
-    for way in range(2):
-        for distance in range(1, reach[way] + 1):
-            cot_aside(way, distance).wait_recv()
-
-    low = lax.broadcasted_iota(jnp.int32, (half, BLOCK), 1) < half
-
-    def lay_cot(zz):
-        first, last = cot_all[2 * zz], cot_all[2 * zz + 1]
-        cot_blk[3 * zz] = first[:BLOCK]
-        cot_blk[3 * zz + 2] = last[:BLOCK]
-        a, b = first[BLOCK:].astype(F32), last[BLOCK:].astype(F32)
-        top = jnp.where(low, a, pltpu.roll(b, half, 1))
-        bottom = jnp.where(low, pltpu.roll(a, half, 1), b)
-        cot_blk[3 * zz + 1] = stack(top, bottom)
-
-    loop(0, chips, lay_cot)
+    def cot_begin():
+        for way in range(2):
+            cot_hop(way, 1).start()
+        for way in range(2):
+            if JUMP <= reach[way]:
+                cot_hop(way, JUMP).start()
+        cot_aside(0, 0).start()
+
+    def cot_end():
+        cot_aside(0, 0).wait_recv()
+        for way in range(2):
+            for distance in range(1, reach[way] + 1):
+                cot_aside(way, distance).wait_recv()
+
+    def w1_begin():
+        z_start("w1")
+        w1_in[core * chips + z] = w1_out[z]
+
+    def lay_mv():
+        for i in (1, 2):
+            local[i].wait()
+
+        def pack_mv(n):
+            k = table[SEND_SLOT, n]
+            mv_out[n] = stack(own_rows(1, k), own_rows(2, k))
+
+        loop_by(4, owners, pack_mv)
+        mv_in[core * chips + z] = mv_out[pl.ds(2 * z, 2)]
+
+    def lay_hid():
+        for r in range(row_share):
+            block = hid[:, r * BLOCK : (r + 1) * BLOCK]
+            hid_b[r] = block
+            hid_t[r] = block.astype(F32).T.astype(BF16)
+        prod[owners] = jnp.zeros(prod.shape[1:], F32)
+
+    def w2_begin():
+        def pack_w2(k):
+            parts = []
+            for r in (2 * k, 2 * k + 1):
+                parts.append(core_rows(w1_in[table[HOP_OLD, r]]) * table[HOP_KEPT, r].astype(F32))
+            w2_out[k] = stack(*parts)
+
+        loop_by(4, chips, pack_w2)
+        z_start("w2")
+        w2_in[core * chips + z] = w2_out[z]
 
     def grad_pair(k):
         slices = []
         for n in (2 * k, 2 * k + 1):
-            g = jnp.dot(hid_t[table[ROW_ROW, n]], cot_blk[table[ROW_COL, n]], preferred_element_type=F32)
+            at = table[ROW_COL, n] * 2
+            cot_t = jnp.concatenate([cot_all[at], cot_all[at + 1]], 0)
+            g = lax.dot_general(
+                hid_t[table[ROW_ROW, n]], cot_t, (((1,), (1,)), ((), ())), preferred_element_type=F32
+            )
             slices.append((g * scale).reshape(toks, ROWS, BLOCK))
         g_out[:, k] = jnp.concatenate(slices, 1).astype(BF16)
-
-    loop(0, pairs, grad_pair)
 
     def half_pairs(h):
         return pl.ds(h * (pairs // 2), pairs // 2)
@@ -436,32 +441,16 @@
         for h in range(2):
             loop(1, side, lambda d: do(g_first(h, 0, d)))
 
-    g_each(lambda copy: copy.start())
-
-    fwd["mv"].wait_recv()
-
-    def pack_state(p):
-        parts = []
-        for s in (2 * p, 2 * p + 1):
-            kept = table[NEW_KEPT, s].astype(F32)
-            place = table[NEW_OLD, s]
-            both = mv_in[place, core].astype(F32) * kept
-            parts.append((core_rows(w1_in[place]) * kept, both[:ROWS], both[ROWS:]))
-        for i in range(3):
-            state[t, i * half_dev + p] = stack(parts[0][i], parts[1][i])
-
-    loop(0, half_dev, pack_state)
-
-    z_wait("w2")
-    fwd["w2"].wait_recv()
-
-    def pack_w(k):
-        w_all[t, k] = stack(core_rows(w2_in[k]), core_rows(w2_in[chips + k]))
-
-    loop(0, pairs, pack_w)
-    ag_start(*ag_w)
-    ag_pass_on(*ag_w)
-    ag_start(*ag_state)
+    def g_begin():
+        loop_by(4, pairs, grad_pair)
+        g_each(lambda copy: copy.start())
+
+    def w_begin():
+        def pack_w(k):
+            w_all[t, k] = stack(core_rows(w2_in[k]), core_rows(w2_in[chips + k]))
+
+        loop_by(4, pairs, pack_w)
+        ag_start(*ag_w)
 
     def g_middle(e):
         for h in range(2):
@@ -475,19 +464,33 @@
         for h in range(2):
             g_second(h, e).start()
 
-    loop(1, side, g_on)
-    g_middle(0)
-    for h in range(2):
-        loop(1, side, lambda e: g_second(h, e).wait_recv())
-        total = g_mid[h, 0].astype(F32)
-        for e in range(1, side):
-            total += g_two[h, e].astype(F32)
-        g_sum[half_pairs(h)] = total.astype(BF16)
-    z_start("g")
-    g_new[core * chips + z] = g_sum[z]
-    ag_pass_on(*ag_state)
-
-    ag_wait(*ag_w)
+    def g_pass_on():
+        loop(1, side, g_on)
+
+    def gz_begin():
+        g_middle(0)
+        for h in range(2):
+            loop(1, side, lambda e: g_second(h, e).wait_recv())
+            total = g_mid[h, 0].astype(F32)
+            for e in range(1, side):
+                total += g_two[h, e].astype(F32)
+            g_sum[half_pairs(h)] = total.astype(BF16)
+        z_start("g")
+        g_new[core * chips + z] = g_sum[z]
+
+    def state_begin():
+        def pack_state(p):
+            parts = []
+            for s in (2 * p, 2 * p + 1):
+                kept = table[NEW_KEPT, s].astype(F32)
+                place = table[NEW_OLD, s]
+                both = mv_in[place, core].astype(F32) * kept
+                parts.append((core_rows(w1_in[place]) * kept, both[:ROWS], both[ROWS:]))
+            for i in range(3):
+                state[t, i * half_dev + p] = stack(parts[0][i], parts[1][i])
+
+        loop_by(4, half_dev, pack_state)
+        ag_start(*ag_state)
 
     def product(k):
         both = w_all[:, k].astype(F32)
@@ -497,8 +500,6 @@
             p = jnp.dot(hid_b[table[ROW_ROW, n]], w, preferred_element_type=F32) * scale
             prod[n] = p.reshape(2, half, BLOCK)
 
-    loop(0, pairs, product)
-
     def gather_part(h):
         def column(c):
             total = prod[table[CELL, c], h]
@@ -506,13 +507,14 @@
                 total += prod[table[CELL + r, c], h]
             part[h, c] = total.astype(BF16)
 
-        loop(0, cols, column)
-
-    gather_part(1 - core)
+        loop_by(4, cols, column)
+
     swap = remote(part.at[1 - core], part_sib, fwd_send.at[4], fwd_recv.at[4], sibling)
-    swap.start()
-    gather_part(core)
-    swap.wait_recv()
+
+    def part_begin():
+        loop_by(4, pairs, product)
+        gather_part(1 - core)
+        swap.start()
 
     def term(zz):
         at = pl.ds((zz % chips) * chunk, chunk)
@@ -546,23 +548,24 @@
             if JUMP - 1 - k >= 1:
                 rs_step(way, min(JUMP - 1, reach[way]) - k)
 
-    rs_round(0)
-
-    z_wait("g")
-    fwd["g"].wait_recv()
-
-    def pack_g(p):
-        g_all[t, p] = stack(*[core_rows(g_new[table[NEW_ROW, s]]) for s in (2 * p, 2 * p + 1)])
-
-    loop(0, half_dev, pack_g)
-    ag_start(*ag_g)
-    rs_round(1)
-    ag_pass_on(*ag_g)
-    rs_round(2)
-    rs_round(3)
-
-    ag_wait(*ag_state)
-    ag_wait(*ag_g)
+    finish = remote(fin.at[core], fin.at[core], fwd_send.at[5], fwd_recv.at[5], sibling)
+
+    def rs_end():
+        value = term(z)
+        for way in range(2):
+            for distance in (1, JUMP):
+                if distance <= reach[way]:
+                    rs_hop(way, distance).wait_recv()
+                    value += rs_in[way, distance].astype(F32)
+        fin[core] = value.astype(BF16)
+        finish.start()
+
+    def ga_begin():
+        def pack_g(p):
+            g_all[t, p] = stack(*[core_rows(g_new[table[NEW_ROW, s]]) for s in (2 * p, 2 * p + 1)])
+
+        loop_by(4, half_dev, pack_g)
+        ag_start(*ag_g)
 
     def adam(p):
         g, w, m, v = [
@@ -574,17 +577,48 @@
                 part_rows = value[:, i * ROWS : (i + 1) * ROWS]
                 result[2 * p + i] = part_rows.reshape(BLOCK, BLOCK).astype(BF16)
 
-    loop(0, half_dev, adam)
-
-    value = term(z)
-    for way in range(2):
-        for distance in (1, JUMP):
-            if distance <= reach[way]:
-                rs_hop(way, distance).wait_recv()
-                value += rs_in[way, distance].astype(F32)
-    fin[core] = value.astype(BF16)
-    finish = remote(fin.at[core], fin.at[core], fwd_send.at[5], fwd_recv.at[5], sibling)
-    finish.start()
+    cot_begin()
+    w1_begin()
+    lay_mv()
+    lay_hid()
+    cot_step(1)
+    z_wait("w1")
+    cot_step(5)
+    fwd["w1"].wait_recv()
+    w2_begin()
+    for distance in (2, 6, 3, 7):
+        cot_step(distance)
+    z_wait("w2")
+    cot_step(4)
+    fwd["w2"].wait_recv()
+    w_begin()
+    cot_step(8)
+    z_start("mv")
+    ag_pass_on(*ag_w)
+    cot_end()
+    g_begin()
+    g_pass_on()
+    z_wait("mv")
+    ag_wait(*ag_w)
+    part_begin()
+    gather_part(core)
+    gz_begin()
+    fwd["mv"].wait_recv()
+    state_begin()
+    swap.wait_recv()
+    rs_round(0)
+    ag_pass_on(*ag_state)
+    rs_round(1)
+    z_wait("g")
+    rs_round(2)
+    fwd["g"].wait_recv()
+    ga_begin()
+    rs_round(3)
+    ag_pass_on(*ag_g)
+    rs_end()
+    ag_wait(*ag_state)
+    ag_wait(*ag_g)
+    loop_by(2, half_dev, adam)
     finish.wait_recv()
     out_y[...] = fin[...]
 
@@ -620,22 +654,17 @@
     half = block // 2
     scale = (total * block * block / width) ** (-0.5)
 
-    lists = jnp.concatenate([new_owner[:, None], old_blocks, new_blocks], axis=1)
+    vmem = pl.BlockSpec(memory_space=pltpu.VMEM)
+    hbm = pl.BlockSpec(memory_space=pltpu.HBM)
     table = pl.pallas_call(
-        functools.partial(table_kernel, owners, per_dev, row_share),
+        functools.partial(table_kernel, owners, per_dev, row_share, cols),
         out_shape=jax.ShapeDtypeStruct((TABLE_ROWS, 128), jnp.int32),
-        in_specs=[pl.BlockSpec(memory_space=pltpu.VMEM)],
-        out_specs=pl.BlockSpec(memory_space=pltpu.VMEM),
+        in_specs=[vmem, vmem, vmem],
+        out_specs=vmem,
         compiler_params=pltpu.CompilerParams(vmem_limit_bytes=32 * 2**20),
         name="block_table",
-    )(lists)
-
-    whole = jnp.where(core == 0, grad_out[:, :block], grad_out[:, half:])
-    part = jnp.where(core == 0, grad_out[:, block:], grad_out[:, :half])
-    cot = jnp.concatenate([whole, jnp.concatenate([part[:half], part[half:]], 1)], 0)
-
-    vmem = pl.BlockSpec(memory_space=pltpu.VMEM)
-    hbm = pl.BlockSpec(memory_space=pl.ANY)
+    )(new_owner, old_blocks.T, new_blocks.T)
+
     dma = pltpu.SemaphoreType.DMA
     ring = chips // 2
     piece = (chunk, half, block)
@@ -655,8 +684,7 @@
             pltpu.VMEM((owners, 16, block), BF16),
             pltpu.VMEM((owners, 16, block), BF16),
             pltpu.VMEM((owners, 2, 16, block), BF16),
-            pltpu.VMEM((owners, block + half, block), BF16),
-            pltpu.VMEM((cols, tokens, block), BF16),
+            pltpu.VMEM((2 * cols, half, tokens), BF16),
             pltpu.VMEM((row_share, tokens, block), BF16),
             pltpu.VMEM((row_share, block, tokens), BF16),
             pltpu.VMEM((toks, chips, 16, block), BF16),
@@ -689,10 +717,10 @@
             dma((2, ring + 1)),
         ],
         compiler_params=pltpu.CompilerParams(
-            collective_id=0, has_side_effects=True, vmem_limit_bytes=48 * 2**20
+            collective_id=0, has_side_effects=True, vmem_limit_bytes=60 * 2**20
         ),
         name="projection_step",
-    )(table, cot, hidden, old_weight, old_first, old_second)
+    )(table, grad_out.T, hidden, old_weight, old_first, old_second)
 
     y = y.transpose(0, 2, 1, 3).reshape(tokens, chunk * block)
     output = lax.dynamic_slice_in_dim(y, core * grad_out.shape[1], grad_out.shape[1], 1)

time: 118 us -> 104 us (0.88)
  Pallas kernels: 109 us -> 94.6 us
    pallas_call x1, Pallas kernels: 107 us -> 93.9 us  [local(): pl.pallas_call(functools.partial(step_kernel, scale), out_shape=(jax.Shap...]
    unnamed x19 -> x17, local copies, waits for them, and re-layouts: 6.12 us -> 6.49 us
where the time goes in v3:
time: 104 us; the launch traced here: 103 us
  Pallas kernels  94.6 us (91%)
  local copies, waits for them, and re-layouts  7.57 us (7%)
    pallas_call x1, Pallas kernels, local(): pl.pallas_call(functools.partial(step_kernel, scale), out_shape=(jax.Shap...  93.9 us
    unnamed x17, local copies, waits for them, and re-layouts  6.49 us

profile of v3, /device:TPU:1, one launch (start us, length us, event | category | flops | bytes accessed | tf_op | source)
XLA Modules:
  0.0 102.8 jit_solution(702637666721218195)
XLA Ops:
  0.6 0.0 copy-start.3
  0.7 0.0 copy-start.2
  0.7 0.0 copy-start.1
  0.7 0.6 copy-done.3
  1.3 0.0 copy-done.2
  1.3 0.0 copy-done.1
  1.4 0.7 block_table.1.table
  2.0 0.0 copy-start
  2.1 0.6 copy-done
  2.7 93.9 %projection_step.1 = (bf16[2,3,64,128]{3,2,1,0:T(8,128)(2,1)}, bf16[24,128,128]{2,1,0:T(8,128)(2,1)}, bf16[24,128,128]{2,1,0:T(8,128)(2,1)}, bf16[24,128,128]{2,1,0:T(8,128)(2,1)}) custom-call(s32[16,128]{1,0:T(8,128)} %copy-done, bf16[192,128]{1,0:T(8,128)(2,1)} %bitcast.14, bf16[128,768]{1,0:T(8,128)(2,1)} %hid.1, bf16[24,128,128]{2,1,0:T(8,128)(2,1)} %old_w.1, ...), custom_call_target="tpu_custom_call" | custom-call | tf_op jit(solution)/shard_map/projection_step/pallas_call | solution.py:672
  96.5 1.0 copy.12
  97.5 0.1 constant_dynamic-slice_fusion
  97.6 0.7 copy.13
  98.4 0.0 copy-start.5
  98.4 2.2 %copy.20 = bf16[24,128,128]{2,1,0:T(8,128)(2,1)} copy(bf16[24,128,128]{2,1,0:T(8,128)(2,1)} %get-tuple-element.21) | data formatting | bytes 1572864
  100.5 0.0 copy-done.5
  100.5 0.0 copy-start.4
  100.5 0.9 copy.21
  101.4 0.5 copy-done.4
  102.0 0.9 copy.22
  (1 shorter events, 0.0 us)
Async XLA Ops:
  0.6 0.7 copy-start.3
  0.7 0.7 copy-start.2
  0.7 0.7 copy-start.1
  2.0 0.6 copy-start
  98.4 2.2 %copy-start.5 = (bf16[24,128,128]{2,1,0:T(8,128)(2,1)S(1)}, bf16[24,128,128]{2,1,0:T(8,128)(2,1)}, u32[]{:S(2)}) copy-start(bf16[24,128,128]{2,1,0:T(8,128)(2,1)} %get-tuple-element.22) | copy-start | bytes 2359300
  100.5 1.4 %copy-start.4 = (bf16[24,128,128]{2,1,0:T(8,128)(2,1)S(1)}, bf16[24,128,128]{2,1,0:T(8,128)(2,1)}, u32[]{:S(2)}) copy-start(bf16[24,128,128]{2,1,0:T(8,128)(2,1)} %get-tuple-element.23) | copy-start | bytes 2359300

commit v4 on v3

--- a/solution.py
+++ b/solution.py
@@ -30,7 +30,14 @@
 TABLE_ROWS = 16
 
 
-def table_kernel(owners, per_dev, row_share, cols, owner_ref, old_ref, new_ref, table_ref):
+def table_kernel(owners, per_dev, row_share, cols, owner_ref, old_ref, new_ref, *refs):
+    olds, table_ref, mine_refs, sem = refs[:3], refs[3], refs[4:7], refs[7]
+    rows = pl.ds((lax.axis_index("tok") // 2) * 16, 16)
+    copies = [
+        pltpu.make_async_copy(old.at[:, rows, :], ref, sem.at[i]) for i, (old, ref) in enumerate(zip(olds, mine_refs))
+    ]
+    for copy in copies:
+        copy.start()
     me = lax.axis_index("own")
     total = owner_ref.shape[0]
     shape = (cols, total)
@@ -93,6 +100,8 @@
         turned = jnp.where(lane == row, value.astype(F32), turned)
     turned = jnp.concatenate([turned, jnp.zeros((128 - cols, 128), F32)], 0).T
     table_ref[...] = turned[:TABLE_ROWS].astype(jnp.int32)
+    for copy in copies:
+        copy.wait()
 
 
 def adam_update(weight, first, second, grad):
@@ -102,6 +111,8 @@
     return weight - change, moment, square
 
 
+TABLE_VMEM = 53
+STEP_VMEM = 48
 JUMP = 5
 
 
@@ -110,16 +121,12 @@
     table,
     cot,
     hid,
-    old_w,
-    old_m,
-    old_v,
-    out_y,
-    out_w,
-    out_m,
-    out_v,
     loc_w,
     loc_m,
     loc_v,
+    fin,
+    g_all,
+    state,
     w1_out,
     w1_in,
     w2_out,
@@ -135,16 +142,12 @@
     g_two,
     g_sum,
     g_new,
-    g_all,
     w_all,
-    state,
     prod,
     part,
     part_sib,
     rs_out,
     rs_in,
-    fin,
-    loc_sem,
     cot_send,
     cot_recv,
     sib_send,
@@ -165,7 +168,7 @@
     z, core = o // 2, o % 2
     y, x = t // side, t % side
     sibling = {"tok": t, "own": z * 2 + 1 - core}
-    per_dev = old_w.shape[0]
+    per_dev = loc_w.shape[0]
     half_dev = per_dev // 2
     row_share = hid_t.shape[0]
     cols = part.shape[1]
@@ -205,13 +208,6 @@
 
         loop(0, last // n, several)
 
-    rows = pl.ds((t // 2) * 16, 16)
-    local = [
-        pltpu.make_async_copy(old.at[:, rows, :], loc[i], loc_sem.at[i])
-        for i, old in enumerate((old_w, old_m, old_v))
-    ]
-    for copy in local:
-        copy.start()
     barrier = pltpu.get_barrier_semaphore()
 
     def greet(device):
@@ -240,7 +236,6 @@
 
     for i in range(units):
         cot_all[o * units + i] = cot[i * half : (i + 1) * half, :]
-    local[0].wait()
 
     def pack_w1(k):
         w1_out[k] = stack(own_rows(0, table[SEND_SLOT, 2 * k]), own_rows(0, table[SEND_SLOT, 2 * k + 1]))
@@ -374,9 +369,6 @@
         w1_in[core * chips + z] = w1_out[z]
 
     def lay_mv():
-        for i in (1, 2):
-            local[i].wait()
-
         def pack_mv(n):
             k = table[SEND_SLOT, n]
             mv_out[n] = stack(own_rows(1, k), own_rows(2, k))
@@ -442,7 +434,7 @@
             loop(1, side, lambda d: do(g_first(h, 0, d)))
 
     def g_begin():
-        loop_by(4, pairs, grad_pair)
+        loop_by(8, pairs, grad_pair)
         g_each(lambda copy: copy.start())
 
     def w_begin():
@@ -507,12 +499,12 @@
                 total += prod[table[CELL + r, c], h]
             part[h, c] = total.astype(BF16)
 
-        loop_by(4, cols, column)
+        loop_by(8, cols, column)
 
     swap = remote(part.at[1 - core], part_sib, fwd_send.at[4], fwd_recv.at[4], sibling)
 
     def part_begin():
-        loop_by(4, pairs, product)
+        loop_by(8, pairs, product)
         gather_part(1 - core)
         swap.start()
 
@@ -566,16 +558,6 @@
 
         loop_by(4, half_dev, pack_g)
         ag_start(*ag_g)
-
-    def adam(p):
-        g, w, m, v = [
-            ref[:, i].astype(F32)
-            for ref, i in ((g_all, p), (state, p), (state, half_dev + p), (state, 2 * half_dev + p))
-        ]
-        for result, value in zip((out_w, out_m, out_v), adam_update(w, m, v, g)):
-            for i in range(2):
-                part_rows = value[:, i * ROWS : (i + 1) * ROWS]
-                result[2 * p + i] = part_rows.reshape(BLOCK, BLOCK).astype(BF16)
 
     cot_begin()
     w1_begin()
@@ -618,9 +600,7 @@
     rs_end()
     ag_wait(*ag_state)
     ag_wait(*ag_g)
-    loop_by(2, half_dev, adam)
     finish.wait_recv()
-    out_y[...] = fin[...]
 
     cot_aside(0, 0).wait_send()
     for way in range(2):
@@ -640,10 +620,34 @@
     finish.wait_send()
 
 
+def finish_kernel(step_pairs, y, g_all, state, out_y, out_w, out_m, out_v, turned):
+    half_dev = g_all.shape[1]
+    step = pl.program_id(0)
+
+    @pl.when(step == 0)
+    def _():
+        for j in range(y.shape[1]):
+            block = jnp.concatenate([y[0, j], y[1, j]], 0).astype(F32)
+            turned[j * BLOCK : (j + 1) * BLOCK, :] = block.T
+        width = out_y.shape[0]
+        at = pl.ds(pl.multiple_of((lax.axis_index("own") % 2) * width, BLOCK // 2), width)
+        out_y[...] = turned[at, :].astype(BF16)
+
+    for j in range(step_pairs):
+        p = step * step_pairs + j
+        g, w, m, v = [
+            ref[:, i].astype(F32)
+            for ref, i in ((g_all, p), (state, p), (state, half_dev + p), (state, 2 * half_dev + p))
+        ]
+        for result, value in zip((out_w, out_m, out_v), adam_update(w, m, v, g)):
+            for i in range(2):
+                part_rows = value[:, i * ROWS : (i + 1) * ROWS]
+                result[2 * j + i] = part_rows.reshape(BLOCK, BLOCK).astype(BF16)
+
+
 def local(hidden, grad_out, old_weight, old_first, old_second, old_blocks, new_blocks, new_owner):
     owners, toks = lax.axis_size("own"), lax.axis_size("tok")
     chips = owners // 2
-    core = lax.axis_index("own") % 2
     per_dev, block = old_weight.shape[0], old_weight.shape[1]
     total = new_owner.shape[0]
     tokens = hidden.shape[0]
@@ -656,28 +660,30 @@
 
     vmem = pl.BlockSpec(memory_space=pltpu.VMEM)
     hbm = pl.BlockSpec(memory_space=pltpu.HBM)
-    table = pl.pallas_call(
+    mine = jax.ShapeDtypeStruct((per_dev, 16, block), BF16)
+    table, *locs = pl.pallas_call(
         functools.partial(table_kernel, owners, per_dev, row_share, cols),
-        out_shape=jax.ShapeDtypeStruct((TABLE_ROWS, 128), jnp.int32),
-        in_specs=[vmem, vmem, vmem],
-        out_specs=vmem,
-        compiler_params=pltpu.CompilerParams(vmem_limit_bytes=32 * 2**20),
+        out_shape=(jax.ShapeDtypeStruct((TABLE_ROWS, 128), jnp.int32), mine, mine, mine),
+        in_specs=[vmem, vmem, vmem, hbm, hbm, hbm],
+        out_specs=(vmem,) * 4,
+        scratch_shapes=[pltpu.SemaphoreType.DMA((3,))],
+        compiler_params=pltpu.CompilerParams(vmem_limit_bytes=TABLE_VMEM * 2**20),
         name="block_table",
-    )(new_owner, old_blocks.T, new_blocks.T)
+    )(new_owner, old_blocks.T, new_blocks.T, old_weight, old_first, old_second)
 
     dma = pltpu.SemaphoreType.DMA
     ring = chips // 2
     piece = (chunk, half, block)
-    state_shape = jax.ShapeDtypeStruct(old_weight.shape, BF16)
-    y, new_weight, new_first, new_second = pl.pallas_call(
+    y, g_all, state = pl.pallas_call(
         functools.partial(step_kernel, scale),
-        out_shape=(jax.ShapeDtypeStruct((2,) + piece, BF16), state_shape, state_shape, state_shape),
-        in_specs=[pl.BlockSpec(memory_space=pltpu.SMEM), vmem, vmem, hbm, hbm, hbm],
-        out_specs=(vmem, vmem, vmem, vmem),
+        out_shape=(
+            jax.ShapeDtypeStruct((2,) + piece, BF16),
+            jax.ShapeDtypeStruct((toks, per_dev // 2, 16, block), BF16),
+            jax.ShapeDtypeStruct((toks, 3 * per_dev // 2, 16, block), BF16),
+        ),
+        in_specs=[pl.BlockSpec(memory_space=pltpu.SMEM)] + [vmem] * 5,
+        out_specs=(vmem,) * 3,
         scratch_shapes=[
-            pltpu.VMEM((per_dev, 16, block), BF16),
-            pltpu.VMEM((per_dev, 16, block), BF16),
-            pltpu.VMEM((per_dev, 16, block), BF16),
             pltpu.VMEM((chips, 16, block), BF16),
             pltpu.VMEM((owners, 16, block), BF16),
             pltpu.VMEM((chips, 16, block), BF16),
@@ -693,16 +699,12 @@
             pltpu.VMEM((2, 4, chips // 2, 16, block), BF16),
             pltpu.VMEM((chips, 16, block), BF16),
             pltpu.VMEM((owners, 16, block), BF16),
-            pltpu.VMEM((toks, per_dev // 2, 16, block), BF16),
             pltpu.VMEM((toks, chips, 16, block), BF16),
-            pltpu.VMEM((toks, 3 * per_dev // 2, 16, block), BF16),
             pltpu.VMEM((owners + 1, 2, half, block), F32),
             pltpu.VMEM((2, cols, half, block), BF16),
             pltpu.VMEM((cols, half, block), BF16),
             pltpu.VMEM((2, ring + 1) + piece, BF16),
             pltpu.VMEM((2, ring + 1) + piece, BF16),
-            pltpu.VMEM((2,) + piece, BF16),
-            dma((3,)),
             dma((2, ring + 1)),
             dma((2, ring + 1)),
             dma((2, ring + 1)),
@@ -717,14 +719,25 @@
             dma((2, ring + 1)),
         ],
         compiler_params=pltpu.CompilerParams(
-            collective_id=0, has_side_effects=True, vmem_limit_bytes=60 * 2**20
+            collective_id=0, has_side_effects=True, vmem_limit_bytes=STEP_VMEM * 2**20
         ),
         name="projection_step",
-    )(table, grad_out.T, hidden, old_weight, old_first, old_second)
-
-    y = y.transpose(0, 2, 1, 3).reshape(tokens, chunk * block)
-    output = lax.dynamic_slice_in_dim(y, core * grad_out.shape[1], grad_out.shape[1], 1)
-    return (output, new_weight, new_first, new_second)
+    )(table, grad_out.T, hidden, *locs)
+
+    step_pairs = 4
+    state_spec = pl.BlockSpec((2 * step_pairs, block, block), lambda i: (i, 0, 0))
+    state_shape = jax.ShapeDtypeStruct(old_weight.shape, BF16)
+    out, *new_state = pl.pallas_call(
+        functools.partial(finish_kernel, step_pairs),
+        grid=(per_dev // (2 * step_pairs),),
+        out_shape=(jax.ShapeDtypeStruct((grad_out.shape[1], tokens), BF16),) + (state_shape,) * 3,
+        in_specs=[vmem, vmem, vmem],
+        out_specs=(pl.BlockSpec((grad_out.shape[1], tokens), lambda i: (0, 0)),) + (state_spec,) * 3,
+        scratch_shapes=[pltpu.VMEM((chunk * block, tokens), F32)],
+        compiler_params=pltpu.CompilerParams(vmem_limit_bytes=16 * 2**20),
+        name="adam",
+    )(y, g_all, state)
+    return (out.T, *new_state)
 
 
 def solution(mesh):

time: 104 us -> 98.7 us (0.949)
  local copies, waits for them, and re-layouts: 7.57 us -> 2.11 us
  Pallas kernels: 94.6 us -> 95.7 us
    unnamed x17 -> x10, local copies, waits for them, and re-layouts: 6.49 us -> 2.11 us
    pallas_call x0 -> x1, Pallas kernels: none -> 2.79 us  [local(): pl.pallas_call(functools.partial(finish_kernel, step_pairs), grid=(per_de...]
    pallas_call x1, Pallas kernels: 93.9 us -> 91.5 us  [local(): pl.pallas_call(functools.partial(step_kernel, scale), out_shape=(jax.Shap...]
where the time goes in v4:
time: 98.7 us; the launch traced here: 98.5 us
  Pallas kernels  95.7 us (97%)
  local copies, waits for them, and re-layouts  2.11 us (2%)
    pallas_call x1, Pallas kernels, local(): pl.pallas_call(functools.partial(step_kernel, scale), out_shape=(jax.Shap...  91.5 us
    pallas_call x1, Pallas kernels, local(): pl.pallas_call(functools.partial(finish_kernel, step_pairs), grid=(per_de...  2.79 us
    unnamed x10, local copies, waits for them, and re-layouts  2.11 us

profile of v4, /device:TPU:1, one launch (start us, length us, event | category | flops | bytes accessed | tf_op | source)
XLA Modules:
  0.0 98.5 jit_solution(9104816369933189151)
XLA Ops:
  0.6 0.0 copy-start.1
  0.6 0.0 copy-start
  0.7 0.0 copy-start.2
  0.7 0.7 copy-done.2
  1.4 0.0 copy-start.3
  1.4 0.7 copy-done.3
  2.1 0.0 copy-start.4
  2.1 0.7 copy-done.4
  2.8 1.4 %block_table.1 = (s32[16,128]{1,0:T(8,128)S(1)}, bf16[24,16,128]{2,1,0:T(8,128)(2,1)S(1)}, bf16[24,16,128]{2,1,0:T(8,128)(2,1)S(1)}, bf16[24,16,128]{2,1,0:T(8,128)(2,1)S(1)}) custom-call(s32[768]{0:T(1024)S(1)} %copy-done.4, s32[2,768]{1,0:T(2,128)S(1)} %bitcast.5, s32[2,768]{1,0:T(2,128)S(1)} %bitcast.6, bf16[24,128,128]{2,1,0:T(8,128)(2,1)} %refs_0_.1, ...), custom_call_target="tpu_custom_call" | custom-call | tf_op jit(solution)/shard_map/block_table/pallas_call | solution.py:664
  4.1 0.0 copy-done.1
  4.1 0.0 copy-done
  4.1 91.5 %projection_step.1 = (bf16[2,3,64,128]{3,2,1,0:T(8,128)(2,1)S(1)}, bf16[16,12,16,128]{3,2,1,0:T(8,128)(2,1)S(1)}, bf16[16,36,16,128]{3,2,1,0:T(8,128)(2,1)S(1)}) custom-call(s32[16,128]{1,0:T(8,128)S(1)} %get-tuple-element.15.table, bf16[192,128]{1,0:T(8,128)(2,1)S(1)} %bitcast.4, bf16[128,768]{1,0:T(8,128)(2,1)S(1)} %copy-done, ...), custom_call_target="tpu_custom_call" | custom-call | tf_op jit(solution)/shard_map/projection_step/pallas_call | solution.py:677
  95.7 2.8 %adam.1 = (bf16[192,128]{1,0:T(8,128)(2,1)}, bf16[24,128,128]{2,1,0:T(8,128)(2,1)}, bf16[24,128,128]{2,1,0:T(8,128)(2,1)}, bf16[24,128,128]{2,1,0:T(8,128)(2,1)}) custom-call(bf16[2,3,64,128]{3,2,1,0:T(8,128)(2,1)S(1)} %get-tuple-element.19.y, bf16[16,12,16,128]{3,2,1,0:T(8,128)(2,1)S(1)} %get-tuple-element.20.g_all, ...), custom_call_target="tpu_custom_call" | custom-call | tf_op jit(solution)/shard_map/adam/pallas_call | solution.py:730
Async XLA Ops:
  0.6 3.5 %copy-start.1 = (bf16[128,192]{0,1:T(8,128)(2,1)S(1)}, bf16[128,192]{0,1:T(8,128)(2,1)}, u32[]{:S(2)}) copy-start(bf16[128,192]{0,1:T(8,128)(2,1)} %param.9) | copy-start | bytes 147460
  0.6 3.5 %copy-start = (bf16[128,768]{1,0:T(8,128)(2,1)S(1)}, bf16[128,768]{1,0:T(8,128)(2,1)}, u32[]{:S(2)}) copy-start(bf16[128,768]{1,0:T(8,128)(2,1)} %hid.1) | copy-start | bytes 589828
  0.7 0.7 copy-start.2
  1.4 0.7 copy-start.3
  2.1 0.7 copy-start.4

commit v5 on v4

--- a/solution.py
+++ b/solution.py
@@ -30,14 +30,20 @@
 TABLE_ROWS = 16
 
 
-def table_kernel(owners, per_dev, row_share, cols, owner_ref, old_ref, new_ref, *refs):
-    olds, table_ref, mine_refs, sem = refs[:3], refs[3], refs[4:7], refs[7]
+def table_kernel(owners, per_dev, row_share, cols, owner_hbm, old_hbm, new_hbm, *refs):
+    olds, table_ref, mine_refs, (owner_ref, old_ref, new_ref, sem) = refs[:3], refs[3], refs[4:7], refs[7:]
     rows = pl.ds((lax.axis_index("tok") // 2) * 16, 16)
     copies = [
         pltpu.make_async_copy(old.at[:, rows, :], ref, sem.at[i]) for i, (old, ref) in enumerate(zip(olds, mine_refs))
     ]
-    for copy in copies:
+    lists = [
+        pltpu.make_async_copy(src, ref, sem.at[3 + i])
+        for i, (src, ref) in enumerate(((owner_hbm, owner_ref), (old_hbm, old_ref), (new_hbm, new_ref)))
+    ]
+    for copy in lists + copies:
         copy.start()
+    for copy in lists:
+        copy.wait()
     me = lax.axis_index("own")
     total = owner_ref.shape[0]
     shape = (cols, total)
@@ -113,6 +119,7 @@
 
 TABLE_VMEM = 53
 STEP_VMEM = 48
+
 JUMP = 5
 
 
@@ -583,10 +590,10 @@
     z_wait("mv")
     ag_wait(*ag_w)
     part_begin()
+    fwd["mv"].wait_recv()
+    state_begin()
     gather_part(core)
     gz_begin()
-    fwd["mv"].wait_recv()
-    state_begin()
     swap.wait_recv()
     rs_round(0)
     ag_pass_on(*ag_state)
@@ -664,9 +671,14 @@
     table, *locs = pl.pallas_call(
         functools.partial(table_kernel, owners, per_dev, row_share, cols),
         out_shape=(jax.ShapeDtypeStruct((TABLE_ROWS, 128), jnp.int32), mine, mine, mine),
-        in_specs=[vmem, vmem, vmem, hbm, hbm, hbm],
+        in_specs=[hbm] * 6,
         out_specs=(vmem,) * 4,
-        scratch_shapes=[pltpu.SemaphoreType.DMA((3,))],
+        scratch_shapes=[
+            pltpu.VMEM((total,), jnp.int32),
+            pltpu.VMEM((2, total), jnp.int32),
+            pltpu.VMEM((2, total), jnp.int32),
+            pltpu.SemaphoreType.DMA((6,)),
+        ],
         compiler_params=pltpu.CompilerParams(vmem_limit_bytes=TABLE_VMEM * 2**20),
         name="block_table",
     )(new_owner, old_blocks.T, new_blocks.T, old_weight, old_first, old_second)
@@ -724,7 +736,7 @@
         name="projection_step",
     )(table, grad_out.T, hidden, *locs)
 
-    step_pairs = 4
+    step_pairs = 6
     state_spec = pl.BlockSpec((2 * step_pairs, block, block), lambda i: (i, 0, 0))
     state_shape = jax.ShapeDtypeStruct(old_weight.shape, BF16)
     out, *new_state = pl.pallas_call(

time: 98.7 us -> 98 us (level)
  no operation moved by 1% of the time
where the time goes in v5:
time: 98 us; the launch traced here: 97.7 us
  Pallas kernels  94.9 us (97%)
  local copies, waits for them, and re-layouts  2.11 us (2%)
    pallas_call x1, Pallas kernels, local(): pl.pallas_call(functools.partial(step_kernel, scale), out_shape=(jax.Shap...  91.3 us
    pallas_call x1, Pallas kernels, local(): pl.pallas_call(functools.partial(finish_kernel, step_pairs), grid=(per_de...  2.63 us
    unnamed x10, local copies, waits for them, and re-layouts  2.11 us

profile of v5, /device:TPU:1, one launch (start us, length us, event | category | flops | bytes accessed | tf_op | source)
XLA Modules:
  0.0 97.7 jit_solution(343929851489541657)
XLA Ops:
  0.6 0.0 copy-start.1
  0.6 0.0 copy-start
  0.7 0.0 copy-start.2
  0.7 0.7 copy-done.2
  1.4 0.0 copy-start.3
  1.4 0.7 copy-done.3
  2.1 0.0 copy-start.4
  2.1 0.7 copy-done.4
  2.8 1.0 %block_table.1 = (s32[16,128]{1,0:T(8,128)S(1)}, bf16[24,16,128]{2,1,0:T(8,128)(2,1)S(1)}, bf16[24,16,128]{2,1,0:T(8,128)(2,1)S(1)}, bf16[24,16,128]{2,1,0:T(8,128)(2,1)S(1)}) custom-call(s32[768]{0:T(1024)S(1)} %copy-done.4, s32[2,768]{1,0:T(2,128)S(1)} %bitcast.5, s32[2,768]{1,0:T(2,128)S(1)} %bitcast.6, bf16[24,128,128]{2,1,0:T(8,128)(2,1)} %refs_0_.1, ...), custom_call_target="tpu_custom_call" | custom-call | tf_op jit(solution)/shard_map/block_table/pallas_call | solution.py:671
  3.8 0.0 copy-done.1
  3.8 0.0 copy-done
  3.8 91.3 %projection_step.1 = (bf16[2,3,64,128]{3,2,1,0:T(8,128)(2,1)S(1)}, bf16[16,12,16,128]{3,2,1,0:T(8,128)(2,1)S(1)}, bf16[16,36,16,128]{3,2,1,0:T(8,128)(2,1)S(1)}) custom-call(s32[16,128]{1,0:T(8,128)S(1)} %get-tuple-element.15.table, bf16[192,128]{1,0:T(8,128)(2,1)S(1)} %bitcast.4, bf16[128,768]{1,0:T(8,128)(2,1)S(1)} %copy-done, ...), custom_call_target="tpu_custom_call" | custom-call | tf_op jit(solution)/shard_map/projection_step/pallas_call | solution.py:689
  95.1 2.6 %adam.1 = (bf16[192,128]{1,0:T(8,128)(2,1)}, bf16[24,128,128]{2,1,0:T(8,128)(2,1)}, bf16[24,128,128]{2,1,0:T(8,128)(2,1)}, bf16[24,128,128]{2,1,0:T(8,128)(2,1)}) custom-call(bf16[2,3,64,128]{3,2,1,0:T(8,128)(2,1)S(1)} %get-tuple-element.19.y, bf16[16,12,16,128]{3,2,1,0:T(8,128)(2,1)S(1)} %get-tuple-element.20.g_all, ...), custom_call_target="tpu_custom_call" | custom-call | tf_op jit(solution)/shard_map/adam/pallas_call | solution.py:742
Async XLA Ops:
  0.6 3.2 %copy-start.1 = (bf16[128,192]{0,1:T(8,128)(2,1)S(1)}, bf16[128,192]{0,1:T(8,128)(2,1)}, u32[]{:S(2)}) copy-start(bf16[128,192]{0,1:T(8,128)(2,1)} %param.9) | copy-start | bytes 147460
  0.6 3.2 %copy-start = (bf16[128,768]{1,0:T(8,128)(2,1)S(1)}, bf16[128,768]{1,0:T(8,128)(2,1)}, u32[]{:S(2)}) copy-start(bf16[128,768]{1,0:T(8,128)(2,1)} %hid.1) | copy-start | bytes 589828
  0.7 0.7 copy-start.2
  1.4 0.7 copy-start.3
  2.1 0.7 copy-start.4

commit v6 on v5

--- a/solution.py
+++ b/solution.py
@@ -309,7 +309,8 @@
     }
 
     def z_start(name):
-        loop(0, chips - 1, lambda i: z_copy(*z_all[name], far_first(i)).start())
+        for i in range(chips - 1):
+            z_copy(*z_all[name], far_first(i)).start()
 
     def z_wait(name):
         loop(1, chips, lambda d: z_copy(*z_all[name], d).wait_recv())
@@ -327,17 +328,21 @@
 
     def ag_start(plane, at):
         for h in range(2):
-            loop(1, side, lambda d: xy_one(plane, at, h, d).start())
-        for h in range(2):
-            loop(1, side, lambda d: xy_two(plane, at, h, 0, d).start())
+            for d in range(1, side):
+                xy_one(plane, at, h, d).start()
+        for h in range(2):
+            for d in range(1, side):
+                xy_two(plane, at, h, 0, d).start()
 
     def ag_pass_on(plane, at):
         def pass_on(d):
             for h in range(2):
                 xy_one(plane, at, h, d).wait_recv()
-                loop(1, side, lambda dd: xy_two(plane, at, h, side - d, dd).start())
-
-        loop(1, side, pass_on)
+                for dd in range(1, side):
+                    xy_two(plane, at, h, side - d, dd).start()
+
+        for d in (1, 3, 2):
+            pass_on(d)
 
     def ag_each(plane, at, do):
         for h in range(2):

time: 98 us -> 97.5 us (level)
  no operation moved by 1% of the time
where the time goes in v6:
time: 97.5 us; the launch traced here: 97.3 us
  Pallas kernels  94.5 us (97%)
  local copies, waits for them, and re-layouts  2.11 us (2%)
    pallas_call x1, Pallas kernels, local(): pl.pallas_call(functools.partial(step_kernel, scale), out_shape=(jax.Shap...  90.8 us
    pallas_call x1, Pallas kernels, local(): pl.pallas_call(functools.partial(finish_kernel, step_pairs), grid=(per_de...  2.63 us
    unnamed x10, local copies, waits for them, and re-layouts  2.11 us

profile of v6, /device:TPU:1, one launch (start us, length us, event | category | flops | bytes accessed | tf_op | source)
XLA Modules:
  0.0 97.3 jit_solution(3012135258338917178)
XLA Ops:
  0.6 0.0 copy-start.1
  0.6 0.0 copy-start
  0.7 0.0 copy-start.2
  0.7 0.7 copy-done.2
  1.4 0.0 copy-start.3
  1.4 0.7 copy-done.3
  2.1 0.0 copy-start.4
  2.1 0.7 copy-done.4
  2.8 1.0 %block_table.1 = (s32[16,128]{1,0:T(8,128)S(1)}, bf16[24,16,128]{2,1,0:T(8,128)(2,1)S(1)}, bf16[24,16,128]{2,1,0:T(8,128)(2,1)S(1)}, bf16[24,16,128]{2,1,0:T(8,128)(2,1)S(1)}) custom-call(s32[768]{0:T(1024)S(1)} %copy-done.4, s32[2,768]{1,0:T(2,128)S(1)} %bitcast.5, s32[2,768]{1,0:T(2,128)S(1)} %bitcast.6, bf16[24,128,128]{2,1,0:T(8,128)(2,1)} %refs_0_.1, ...), custom_call_target="tpu_custom_call" | custom-call | tf_op jit(solution)/shard_map/block_table/pallas_call | solution.py:676
  3.8 0.0 copy-done.1
  3.8 0.0 copy-done
  3.8 90.8 %projection_step.1 = (bf16[2,3,64,128]{3,2,1,0:T(8,128)(2,1)S(1)}, bf16[16,12,16,128]{3,2,1,0:T(8,128)(2,1)S(1)}, bf16[16,36,16,128]{3,2,1,0:T(8,128)(2,1)S(1)}) custom-call(s32[16,128]{1,0:T(8,128)S(1)} %get-tuple-element.15.table, bf16[192,128]{1,0:T(8,128)(2,1)S(1)} %bitcast.4, bf16[128,768]{1,0:T(8,128)(2,1)S(1)} %copy-done, ...), custom_call_target="tpu_custom_call" | custom-call | tf_op jit(solution)/shard_map/projection_step/pallas_call | solution.py:694
  94.7 2.6 %adam.1 = (bf16[192,128]{1,0:T(8,128)(2,1)}, bf16[24,128,128]{2,1,0:T(8,128)(2,1)}, bf16[24,128,128]{2,1,0:T(8,128)(2,1)}, bf16[24,128,128]{2,1,0:T(8,128)(2,1)}) custom-call(bf16[2,3,64,128]{3,2,1,0:T(8,128)(2,1)S(1)} %get-tuple-element.19.y, bf16[16,12,16,128]{3,2,1,0:T(8,128)(2,1)S(1)} %get-tuple-element.20.g_all, ...), custom_call_target="tpu_custom_call" | custom-call | tf_op jit(solution)/shard_map/adam/pallas_call | solution.py:747
Async XLA Ops:
  0.6 3.2 %copy-start.1 = (bf16[128,192]{0,1:T(8,128)(2,1)S(1)}, bf16[128,192]{0,1:T(8,128)(2,1)}, u32[]{:S(2)}) copy-start(bf16[128,192]{0,1:T(8,128)(2,1)} %param.9) | copy-start | bytes 147460
  0.6 3.2 %copy-start = (bf16[128,768]{1,0:T(8,128)(2,1)S(1)}, bf16[128,768]{1,0:T(8,128)(2,1)}, u32[]{:S(2)}) copy-start(bf16[128,768]{1,0:T(8,128)(2,1)} %hid.1) | copy-start | bytes 589828
  0.7 0.7 copy-start.2
  1.4 0.7 copy-start.3
  2.1 0.7 copy-start.4
